TPU v7x, 1024 devices: a whole 8x8x8 slice. The times are simulated.
1024 devices in a mesh: path: 64 (over z, x), fsdp: 16 (over y, core).
Axes of the slice: x: 8, y: 8, z: 8, core: 2. Of those that a mesh axis runs over, the one named last changes fastest.
Arguments:
- token_pool: bfloat16 [512, 2048], P(None, 'fsdp'), may hold values from -6 to 6
- batch_ids: int32 [64, 1024], P('path'), may hold values from 0 to 511
- module_table: int32 [64], replicated, may hold values from 0 to 15, as said below
- cotangent: bfloat16 [64, 1024, 2048], P('path', None, 'fsdp'), may hold values from -6 to 6
- path_weights: bfloat16 [64, 2048, 2048], P('path', None, 'fsdp'), may hold values from -5 to 5
- first_moment: bfloat16 [64, 2048, 2048], P('path', None, 'fsdp'), may hold values from -2 to 2
- second_moment: bfloat16 [64, 2048, 2048], P('path', None, 'fsdp'), may hold values from 0.0099487305 to 1
- master_weights: float32 [16, 2048, 2048], P(None, 'path', 'fsdp'), may hold values from -5 to 5
- outer_momentum: float32 [16, 2048, 2048], P(None, 'path', 'fsdp'), may hold values from -3 to 3
Outputs:
- new_master: float32 [16, 2048, 2048], P(None, 'path', 'fsdp')
- new_momentum: float32 [16, 2048, 2048], P(None, 'path', 'fsdp')
- first_average: bfloat16 [16, 2048, 2048], P(None, 'path', 'fsdp')
- second_average: bfloat16 [16, 2048, 2048], P(None, 'path', 'fsdp')
Inputs may be any that keep to these rules, and one draw needn't show every extreme that they name: `module_table`: the module each path visits; at least one of the 16 modules is visited by no path.
All inputs are finite; a program needn't handle non-finite values.
Results may differ from a plain program's by a relative error of at most 0.0033.
Values may be sent and summed in bfloat16 or wider, within the bound.
No kernel may reach another device: no remote copies, remote signals or barrier semaphores. Data moves between devices by JAX's collectives and lax.ppermute only.
A program may use at most 32 MiB of HBM per device.

v0:
```python
import jax
import jax.numpy as jnp
from jax import lax
from jax.sharding import PartitionSpec as P

D = 2048


beta_first = 0.9
beta_second = 0.95
inner_rate = 0.05
decay_rate = 0.1
epsilon = 1e-08
nesterov = 0.9
outer_rate = 0.7


def per_device(
    token_pool,
    batch_ids,
    module_table,
    cotangent,
    path_weights,
    first_moment,
    second_moment,
    master_weights,
    outer_momentum,
):
    factor = D ** (-0.5)
    token_ids = batch_ids[0]
    picked = jnp.take(token_pool, token_ids, axis=0)
    tokens_full = lax.all_gather(picked, "fsdp", axis=1, tiled=True)
    weights = path_weights[0]
    pre_act = jnp.dot(tokens_full, weights, preferred_element_type=jnp.float32) * factor
    sigmoid_act = jax.nn.sigmoid(pre_act)
    slope = (
        cotangent[0].astype(jnp.float32) * sigmoid_act * (1.0 + pre_act * (1.0 - sigmoid_act))
    ).astype(jnp.bfloat16)
    gradient = (
        lax.dot_general(
            tokens_full, slope, (((0,), (0,)), ((), ())), preferred_element_type=jnp.float32
        )
        * factor
    )
    moment_one = beta_first * first_moment[0].astype(jnp.float32) + (1.0 - beta_first) * gradient
    moment_two = (
        beta_second * second_moment[0].astype(jnp.float32)
        + (1.0 - beta_second) * gradient * gradient
    )
    weights_old = weights.astype(jnp.float32)
    weights_new = weights_old - inner_rate * (
        moment_one / (jnp.sqrt(moment_two) + epsilon) + decay_rate * weights_old
    )
    groups = lax.axis_size("path")
    rows_own = weights.shape[0] // groups
    columns = weights.shape[1]

    def split_rows(values):
        return values.astype(jnp.bfloat16).reshape(groups, rows_own, columns)

    recv_weights, recv_first, recv_second = (
        lax.all_to_all(split_rows(weights_new), "path", split_axis=0, concat_axis=0, tiled=True),
        lax.all_to_all(split_rows(moment_one), "path", split_axis=0, concat_axis=0, tiled=True),
        lax.all_to_all(split_rows(moment_two), "path", split_axis=0, concat_axis=0, tiled=True),
    )
    labels = jnp.arange(master_weights.shape[0], dtype=jnp.int32)
    member = labels[:, None] == module_table[None, :]
    onehot = member.astype(jnp.bfloat16)
    counts = jnp.sum(member.astype(jnp.int32), axis=1)

    def module_sum(received):
        flat = received.reshape(groups, rows_own * columns)
        return jnp.dot(onehot, flat, preferred_element_type=jnp.float32).reshape(
            master_weights.shape
        )

    sum_weights = module_sum(recv_weights)
    sum_first = module_sum(recv_first)
    sum_second = module_sum(recv_second)
    divisor = jnp.maximum(counts, 1).astype(jnp.float32)[:, None, None]
    used = (counts > 0)[:, None, None]
    delta = jnp.where(used, master_weights - sum_weights / divisor, jnp.zeros_like(master_weights))
    first_average = (sum_first / divisor).astype(jnp.bfloat16)
    second_average = (sum_second / divisor).astype(jnp.bfloat16)
    new_momentum = nesterov * outer_momentum + delta
    new_master = master_weights - outer_rate * (delta + nesterov * new_momentum)
    return (new_master, new_momentum, first_average, second_average)


def solution(mesh):
    in_specs = (
        P(None, "fsdp"),
        P("path", None),
        P(),
        P("path", None, "fsdp"),
        P("path", None, "fsdp"),
        P("path", None, "fsdp"),
        P("path", None, "fsdp"),
        P(None, "path", "fsdp"),
        P(None, "path", "fsdp"),
    )
    out_specs = (
        P(None, "path", "fsdp"),
        P(None, "path", "fsdp"),
        P(None, "path", "fsdp"),
        P(None, "path", "fsdp"),
    )
    return jax.shard_map(
        per_device, mesh=mesh, in_specs=in_specs, out_specs=out_specs, check_vma=False
    )
```

profile of v0, /device:TPU:16, one launch (start us, length us, event | category | flops | bytes accessed | tf_op | source)
XLA Modules:
  0.0 177.9 jit_solution(10165124885517757627)
XLA Ops:
  7.2 0.0 copy-start
  7.2 0.0 all-gather.2.cloned.1.call-start
  7.2 0.7 compare_select_fusion
  7.9 0.7 compare_and_fusion
  8.7 3.2 %gather_fusion = bf16[1024,128]{1,0:T(8,128)(2,1)S(1)} fusion(bf16[512,128]{1,0:T(8,128)(2,1)S(1)} %copy-done, s32[1024]{0:T(1024)S(1)} %broadcast_clamp_fusion), kind=kCustom, calls=%fused_computation | custom fusion | bytes 528384 | tf_op jit(solution)/shard_map/jit(_take)/gather | solution.py:31
  11.9 0.9 broadcast_select_fusion
  12.8 0.0 all-gather.2.cloned.1.call-update
  12.8 0.0 copy-start.3
  12.8 0.0 copy-start.1
  12.8 0.0 copy-start.2
  12.8 65.3 %all-gather.2.cloned.1.call-done = bf16[1024,2048]{1,0:T(8,128)(2,1)} async-done(((bf16[1024,128]{1,0:T(8,128)(2,1)}), bf16[1024,2048]{1,0:T(8,128)(2,1)}) %all-gather.2.cloned.1.call-update) | async-done | bytes 4194320 | tf_op jit(solution)/shard_map/all_gather | solution.py:32
  78.1 9.8 %fusion.17 = (bf16[2048,128]{1,0:T(8,128)(2,1)S(1)}, bf16[2048,128]{1,0:T(8,128)(2,1)S(1)}, bf16[2048,128]{1,0:T(8,128)(2,1)}) fusion(bf16[1,2048,128]{2,1,0:T(8,128)(2,1)} %param.15, bf16[1,2048,128]{2,1,0:T(8,128)(2,1)} %param.14, bf16[1,2048,128]{2,1,0:T(8,128)(2,1)} %param.13, bf16[1024,2048]{1,0:T(8,128)(2,1)} %all-gather.2.cloned.1.call-done, ...), kind=kOutput, calls=%fused_computation.30 | convolution fusion | flops 1080426496 | bytes 7602176 | tf_op jit(solution)/shard_map/dot_general | solution.py:40
  87.9 33.2 %all_to_all.15 = bf16[64,32,128]{2,1,0:T(8,128)(2,1)S(1)} all-to-all(bf16[64,32,128]{2,1,0:T(8,128)(2,1)S(1)} %bitcast.91), channel_id=1, replica_groups=mesh['path'=64,'fsdp'=16] {'path'}, dimensions={0} | all-to-all | bytes 1048576 | tf_op jit(solution)/shard_map/all_to_all | solution.py:62
  121.1 24.4 %all_to_all.16 = bf16[64,32,128]{2,1,0:T(8,128)(2,1)S(1)} all-to-all(bf16[64,32,128]{2,1,0:T(8,128)(2,1)S(1)} %bitcast.90), channel_id=1, replica_groups=mesh['path'=64,'fsdp'=16] {'path'}, dimensions={0} | all-to-all | bytes 1048576 | tf_op jit(solution)/shard_map/all_to_all | solution.py:64
  145.5 5.1 %all-to-all-start.1 = ((bf16[64,32,128]{2,1,0:T(8,128)(2,1)}), bf16[64,32,128]{2,1,0:T(8,128)(2,1)S(1)}, u32[]{:S(2)}, u32[]{:S(2)}) async-start(bf16[64,32,128]{2,1,0:T(8,128)(2,1)} %bitcast.10), calls=%async_computation.1 | async-start | bytes 1048576 | tf_op jit(solution)/shard_map/all_to_all | solution.py:63
  150.7 0.1 convert_reduce_fusion
  150.8 0.5 fusion.24
  151.3 0.8 copy.27
  152.1 0.3 fusion.3
  152.4 0.7 copy.29
  153.1 16.2 %all-to-all-done.1 = bf16[64,32,128]{2,1,0:T(8,128)(2,1)S(1)} async-done(((bf16[64,32,128]{2,1,0:T(8,128)(2,1)}), bf16[64,32,128]{2,1,0:T(8,128)(2,1)S(1)}, u32[]{:S(2)}, u32[]{:S(2)}) %all-to-all-start.1) | async-done | bytes 524320 | tf_op jit(solution)/shard_map/all_to_all | solution.py:63
  169.3 0.3 fusion.2
  169.6 0.7 copy.28
  170.3 0.8 copy.26
  (7 shorter events, 0.0 us)
Async XLA Ops:
  7.2 1.5 copy-start
  7.2 71.0 %all-gather.2.cloned.1.call-start = ((), (), s32[]{:S(2)}) async-start(), calls=%async_computation.3 | async-start | bytes 4456448 | tf_op jit(solution)/shard_map/all_gather | solution.py:32
  12.8 137.8 %copy-start.3 = (s32[64]{0:T(128)S(1)}, s32[64]{0:T(128)}, u32[]{:S(2)}) copy-start(s32[64]{0:T(128)} %param.11) | copy-start | bytes 772
  12.8 138.0 %copy-start.1 = (f32[16,32,128]{2,1,0:T(8,128)S(1)}, f32[16,32,128]{2,1,0:T(8,128)}, u32[]{:S(2)}) copy-start(f32[16,32,128]{2,1,0:T(8,128)} %param.17) | copy-start | bytes 786436
  12.8 138.0 %copy-start.2 = (f32[16,32,128]{2,1,0:T(8,128)S(1)}, f32[16,32,128]{2,1,0:T(8,128)}, u32[]{:S(2)}) copy-start(f32[16,32,128]{2,1,0:T(8,128)} %param.16) | copy-start | bytes 786436
  145.5 23.8 %all-to-all-start.1 = ((bf16[64,32,128]{2,1,0:T(8,128)(2,1)}), bf16[64,32,128]{2,1,0:T(8,128)(2,1)S(1)}, u32[]{:S(2)}, u32[]{:S(2)}) async-start(bf16[64,32,128]{2,1,0:T(8,128)(2,1)} %bitcast.10), calls=%async_computation.1 | async-start | bytes 1048576 | tf_op jit(solution)/shard_map/all_to_all | solution.py:63
Sparse Core Ops, SparseCore 0:
  12.9 65.1 all-gather.1
where the time goes:
time: 178 us
  waiting for transfers between devices  81.6 us (46%)
  blocking collectives  57.6 us (32%)
  between operations  14.1 us (8%)
  matrix products  10.8 us (6%)
  local copies, waits for them, and re-layouts  6.2 us (3%)
  starting transfers between devices  5.14 us (3%)
  other arithmetic  2.46 us (1%)
    all_gather x1, waiting for transfers between devices, per_device(): tokens_full = lax.all_gather(picked, 'fsdp', axis=1, tiled=True)  65.3 us
    all_to_all x1, blocking collectives, per_device(): lax.all_to_all(split_rows(weights_new), 'path', split_axis=0, concat_axis...  33.2 us
    all_to_all x1, blocking collectives, per_device(): lax.all_to_all(split_rows(moment_two), 'path', split_axis=0, concat_axis=...  24.4 us
    all_to_all x1, waiting for transfers between devices, per_device(): lax.all_to_all(split_rows(moment_one), 'path', split_axis=0, concat_axis=...  16.2 us
    dot_general x1, matrix products, per_device(): lax.dot_general(tokens_full, slope, (((0,), (0,)), ((), ())), preferred_e...  9.77 us
    all_to_all x1, starting transfers between devices, per_device(): lax.all_to_all(split_rows(moment_one), 'path', split_axis=0, concat_axis=...  5.11 us
  transfers between devices with their start and end apart: 2, of which 2 were waited for; matrix products, arithmetic and copies ran while one was open for 1% of the time, Pallas kernels for 0%

commit v1 on v0

v1 whole, which is shorter than its diff:
```python
import jax
import jax.numpy as jnp
from jax import lax
from jax.experimental import pallas as pl
from jax.experimental.pallas import tpu as pltpu
from jax.sharding import Mesh
from jax.sharding import PartitionSpec as P

beta_first = 0.9
beta_second = 0.95
inner_rate = 0.05
decay_rate = 0.1
epsilon = 1e-08
nesterov = 0.9
outer_rate = 0.7

MIB = 1 << 20


def split_bf16(values):
    high = values.astype(jnp.bfloat16)
    low = (values - high.astype(jnp.float32)).astype(jnp.bfloat16)
    return high, low


def gradient_kernel(
    core, near, far, onehot, cotangent, weights, first_old, second_old, sent
):
    stations, pool, width = near.shape
    features = 2 * stations * width
    factor = features ** (-0.5)
    mine = core[0]
    pools = []
    product = None
    for held, side in ((near, mine), (far, 1 - mine)):
        rows = jnp.concatenate([held[s] for s in range(stations)], axis=1)
        block = jnp.concatenate([weights[s, side] for s in range(stations)], axis=0)
        part = jnp.dot(rows, block, preferred_element_type=jnp.float32)
        product = part if product is None else product + part
        pools.append(rows)
    both = jnp.concatenate(split_bf16(product * factor), axis=1)
    taken = jnp.dot(onehot[...], both, preferred_element_type=jnp.float32)
    pre_act = taken[:, :width] + taken[:, width:]
    gate = 1.0 / (1.0 + jnp.exp(-pre_act))
    slope = cotangent[...].astype(jnp.float32) * gate * (1.0 + pre_act * (1.0 - gate))
    slope = slope.astype(jnp.bfloat16)
    summed = lax.dot_general(
        slope, onehot[...], (((0,), (0,)), ((), ())), preferred_element_type=jnp.float32
    )
    pair = jnp.concatenate(split_bf16(summed), axis=0)
    for rows, side in zip(pools, (mine, 1 - mine)):
        both = jnp.dot(pair, rows, preferred_element_type=jnp.float32)
        gradient = (both[:width] + both[width:]) * factor
        for s in range(stations):
            block = jnp.transpose(gradient[:, s * width : (s + 1) * width])
            first = first_old[s, side].astype(jnp.float32)
            first = beta_first * first + (1.0 - beta_first) * block
            second = second_old[s, side].astype(jnp.float32)
            second = beta_second * second + (1.0 - beta_second) * block * block
            rows_own = sent.shape[3] // 2
            for part in range(sent.shape[2]):
                at = slice(part * rows_own, (part + 1) * rows_own)
                sent[s, side, part, :rows_own] = first[at].astype(jnp.bfloat16)
                sent[s, side, part, rows_own:] = second[at].astype(jnp.bfloat16)


def module_kernel(
    table, early, late, master, momentum, new_master, new_momentum, first_out, second_out, totals, counts
):
    paths = late.shape[0]
    modules, rows, _ = master.shape
    totals[...] = jnp.zeros_like(totals)

    def clear(k, carry):
        counts[k] = 0
        return carry

    lax.fori_loop(0, modules, clear, 0)

    def visit(p, carry):
        module = table[p]
        counts[module] = counts[module] + 1
        old = early[p].astype(jnp.float32)
        first = late[p, 0:rows].astype(jnp.float32)
        second = late[p, rows : 2 * rows].astype(jnp.float32)
        new = old - inner_rate * (first / (jnp.sqrt(second) + epsilon) + decay_rate * old)
        totals[0, module] += new.astype(jnp.bfloat16).astype(jnp.float32)
        totals[1, module] += first
        totals[2, module] += second
        return carry

    lax.fori_loop(0, paths, visit, 0, unroll=4)

    def finish(k, carry):
        count = counts[k]
        divisor = jnp.maximum(count, 1).astype(jnp.float32)
        old = master[k]
        delta = jnp.where(count > 0, old - totals[0, k] / divisor, jnp.zeros_like(old))
        moved = nesterov * momentum[k] + delta
        new_momentum[k] = moved
        new_master[k] = old - outer_rate * (delta + nesterov * moved)
        first_out[k] = (totals[1, k] / divisor).astype(jnp.bfloat16)
        second_out[k] = (totals[2, k] / divisor).astype(jnp.bfloat16)
        return carry

    lax.fori_loop(0, modules, finish, 0)


def whole(count):
    return [pl.BlockSpec(memory_space=pltpu.VMEM) for _ in range(count)]


def per_device(
    token_pool,
    batch_ids,
    module_table,
    cotangent,
    path_weights,
    first_moment,
    second_moment,
    master_weights,
    outer_momentum,
):
    stations = lax.axis_size("y")
    groups = lax.axis_size("z") * lax.axis_size("x")
    pool, width = token_pool.shape
    features = path_weights.shape[1]
    rows = features // groups
    tokens = batch_ids.shape[1]
    path_axes = ("z", "x")

    near = lax.all_to_all(
        jnp.broadcast_to(token_pool[None], (stations, pool, width)), "y", 0, 0, tiled=True
    )
    far = lax.ppermute(near, "core", [(0, 1), (1, 0)])

    early = lax.all_to_all(
        path_weights[0].reshape(groups, rows, width), path_axes, 0, 0, tiled=True
    )

    onehot = (
        batch_ids[0][:, None] == lax.broadcasted_iota(jnp.int32, (tokens, pool), 1)
    ).astype(jnp.bfloat16)
    core = lax.axis_index("core").astype(jnp.int32).reshape(1)

    sent = pl.pallas_call(
        gradient_kernel,
        out_shape=jax.ShapeDtypeStruct(
            (stations, 2, width // rows, 2 * rows, width), jnp.bfloat16
        ),
        in_specs=[pl.BlockSpec(memory_space=pltpu.SMEM)] + whole(7),
        out_specs=pl.BlockSpec(memory_space=pltpu.VMEM),
        compiler_params=pltpu.CompilerParams(vmem_limit_bytes=32 * MIB),
        cost_estimate=pl.CostEstimate(
            flops=2_000_000_000, bytes_accessed=5 * MIB, transcendentals=tokens * width
        ),
        name="path_gradient",
    )(
        core,
        near,
        far,
        onehot,
        cotangent[0],
        path_weights[0].reshape(stations, 2, width, width),
        first_moment[0].reshape(stations, 2, width, width),
        second_moment[0].reshape(stations, 2, width, width),
    )

    late = lax.all_to_all(sent.reshape(groups, 2 * rows, width), path_axes, 0, 0, tiled=True)

    shape = master_weights.shape
    return pl.pallas_call(
        module_kernel,
        out_shape=(
            jax.ShapeDtypeStruct(shape, jnp.float32),
            jax.ShapeDtypeStruct(shape, jnp.float32),
            jax.ShapeDtypeStruct(shape, jnp.bfloat16),
            jax.ShapeDtypeStruct(shape, jnp.bfloat16),
        ),
        in_specs=[pl.BlockSpec(memory_space=pltpu.SMEM)] + whole(4),
        out_specs=tuple(whole(4)),
        scratch_shapes=[
            pltpu.VMEM((3,) + shape, jnp.float32),
            pltpu.SMEM((shape[0],), jnp.int32),
        ],
        compiler_params=pltpu.CompilerParams(vmem_limit_bytes=32 * MIB),
        cost_estimate=pl.CostEstimate(
            flops=10_000_000, bytes_accessed=4 * MIB, transcendentals=4 * groups * rows * width
        ),
        name="module_update",
    )(module_table, early, late, master_weights, outer_momentum)


def solution(mesh):
    lengths = (8, 8, 8, 2)
    split = Mesh(mesh.devices.reshape(lengths), ("z", "x", "y", "core"))
    path = ("z", "x")
    fsdp = ("y", "core")
    in_specs = (
        P(None, fsdp),
        P(path, None),
        P(),
        P(path, None, fsdp),
        P(path, None, fsdp),
        P(path, None, fsdp),
        P(path, None, fsdp),
        P(None, path, fsdp),
        P(None, path, fsdp),
    )
    out_specs = (P(None, path, fsdp),) * 4
    return jax.shard_map(
        per_device, mesh=split, in_specs=in_specs, out_specs=out_specs, check_vma=False
    )
```

time: 178 us -> 120 us (0.67)
  the two profiles are of different devices: /device:TPU:16 before, /device:TPU:6 now
where the time goes in v1:
time: 120 us
  blocking collectives  71.3 us (59%)
  starting transfers between devices  24.8 us (21%)
  waiting for transfers between devices  12.7 us (11%)
  Pallas kernels  6.81 us (6%)
  local copies, waits for them, and re-layouts  3.26 us (3%)
    all_to_all x1, blocking collectives, per_device(): lax.all_to_all(jnp.broadcast_to(token_pool[None], (stations, pool, width)...  36.1 us
    all_to_all x1, blocking collectives, per_device(): lax.all_to_all(sent.reshape(groups, 2 * rows, width), path_axes, 0, 0, ti...  35.2 us
    all_to_all x1, starting transfers between devices, per_device(): lax.all_to_all(path_weights[0].reshape(groups, rows, width), path_axes, 0...  22.8 us
    all_to_all x1, waiting for transfers between devices, per_device(): lax.all_to_all(path_weights[0].reshape(groups, rows, width), path_axes, 0...  12.7 us
    pallas_call x1, Pallas kernels, per_device(): pl.pallas_call(gradient_kernel, out_shape=jax.ShapeDtypeStruct((stations,...  4.01 us
    pallas_call x1, Pallas kernels, per_device(): pl.pallas_call(module_kernel, out_shape=(jax.ShapeDtypeStruct(shape, jnp....  2.8 us
  transfers between devices with their start and end apart: 2, of which 1 were waited for; matrix products, arithmetic and copies ran while one was open for 0% of the time, Pallas kernels for 3%

profile of v1, /device:TPU:6, one launch (start us, length us, event | category | flops | bytes accessed | tf_op | source)
XLA Modules:
  0.0 119.9 jit_solution(6318196755278697788)
XLA Ops:
  0.6 1.0 broadcast_in_dim.2
  1.7 36.1 %all_to_all.15.near = bf16[8,512,128]{2,1,0:T(8,128)(2,1)S(1)} all-to-all(bf16[8,512,128]{2,1,0:T(8,128)(2,1)S(1)} %broadcast_in_dim.2), channel_id=1, replica_groups=mesh['z'=8,'x'=8,'y'=8,'core'=2] {'y'}, dimensions={0} | all-to-all | bytes 2097152 | tf_op jit(solution)/shard_map/all_to_all | solution.py:132
  37.8 0.0 copy-start.8
  37.8 2.0 %collective-permute-start = (bf16[8,512,128]{2,1,0:T(8,128)(2,1)S(1)}, bf16[8,512,128]{2,1,0:T(8,128)(2,1)S(1)}, u32[]{:S(2)}, u32[]{:S(2)}) collective-permute-start(bf16[8,512,128]{2,1,0:T(8,128)(2,1)S(1)} %all_to_all.15.near), channel_id=1, source_target_pairs={{0,1},{1,0},{2,3},{3,2},{4,5},{5,4},{6,7},{7,6},{8,9},{9,8},{10,11... | collective-permute-start | bytes 3145736 | tf_op jit(solution)/shard_map/ppermute | solution.py:135
  39.8 0.0 copy-start.5
  39.8 0.0 copy-start.7
  39.8 22.8 %all-to-all-start = ((bf16[64,32,128]{2,1,0:T(8,128)(2,1)}), bf16[64,32,128]{2,1,0:T(8,128)(2,1)S(1)}, u32[]{:S(2)}, u32[]{:S(2)}) async-start(bf16[64,32,128]{2,1,0:T(8,128)(2,1)} %bitcast), calls=%async_computation | async-start | bytes 1048576 | tf_op jit(solution)/shard_map/all_to_all | solution.py:137
  62.6 0.0 copy-start.6
  62.6 0.0 copy-done.8
  62.7 0.2 fusion.onehot
  62.9 0.0 collective-permute-done.far
  62.9 0.0 copy-start.3
  62.9 1.0 copy-done.3
  63.9 0.0 copy-done.5
  63.9 0.0 copy-done.7
  63.9 0.0 copy-done.6
  63.9 1.2 %copy-done.4 = bf16[8,512,128]{2,1,0:T(8,128)(2,1)S(1)} copy-done((bf16[8,512,128]{2,1,0:T(8,128)(2,1)S(1)}, bf16[8,512,128]{2,1,0:T(8,128)(2,1)}, u32[]{:S(2)}) %copy-start.4) | copy-done | bytes 1048600
  65.1 4.0 %path_gradient.1 = bf16[8,2,4,64,128]{4,3,2,1,0:T(8,128)(2,1)S(1)} custom-call(s32[1]{0:T(128)} %bitcast.1.core, bf16[8,512,128]{2,1,0:T(8,128)(2,1)S(1)} %all_to_all.15.near, bf16[8,512,128]{2,1,0:T(8,128)(2,1)S(1)} %copy-done.4, bf16[1024,512]{1,0:T(8,128)(2,1)S(1)} %fusion.onehot, bf16[1024,128]{1,0:T(8,128)(2,1)S(1)} %bitcast.11, ...), custom_call_target="tpu_custom_call" | custom-call | flops 2000000000 | bytes 5242880 | tf_op jit(solution)/shard_map/path_gradient/pallas_call | solution.py:146
  69.1 12.7 %all-to-all-done.early = bf16[64,32,128]{2,1,0:T(8,128)(2,1)S(1)} async-done(((bf16[64,32,128]{2,1,0:T(8,128)(2,1)}), bf16[64,32,128]{2,1,0:T(8,128)(2,1)S(1)}, u32[]{:S(2)}, u32[]{:S(2)}) %all-to-all-start) | async-done | bytes 524320 | tf_op jit(solution)/shard_map/all_to_all | solution.py:137
  81.9 35.2 %all_to_all.16.late = bf16[64,64,128]{2,1,0:T(8,128)(2,1)S(1)} all-to-all(bf16[64,64,128]{2,1,0:T(8,128)(2,1)S(1)} %bitcast.8), channel_id=1, replica_groups=mesh['z'=8,'x'=8,'y'=8,'core'=2] {'z','x'}, dimensions={0} | all-to-all | bytes 2097152 | tf_op jit(solution)/shard_map/all_to_all | solution.py:169
  117.1 0.0 copy-done
  117.1 0.0 copy-done.1
  117.1 0.0 copy-done.2
  117.1 2.8 %module_update.1 = (f32[16,32,128]{2,1,0:T(8,128)}, f32[16,32,128]{2,1,0:T(8,128)}, bf16[16,32,128]{2,1,0:T(8,128)(2,1)}, bf16[16,32,128]{2,1,0:T(8,128)(2,1)}) custom-call(s32[64]{0:T(128)S(1)} %copy-done.2, bf16[64,32,128]{2,1,0:T(8,128)(2,1)S(1)} %all-to-all-done.early, bf16[64,64,128]{2,1,0:T(8,128)(2,1)S(1)} %all_to_all.16.late, ...), custom_call_target="tpu_custom_call" | custom-call | flops 10000000 | bytes 4194304 | tf_op jit(solution)/shard_map/module_update/pallas_call | solution.py:172
  (4 shorter events, 0.0 us)
Async XLA Ops:
  37.8 24.9 %copy-start.8 = (s32[1,1024]{1,0:T(1,128)S(1)}, s32[1,1024]{1,0:T(1,128)}, u32[]{:S(2)}) copy-start(s32[1,1024]{1,0:T(1,128)} %param.10) | copy-start | bytes 12292
  37.8 25.1 %collective-permute-start = (bf16[8,512,128]{2,1,0:T(8,128)(2,1)S(1)}, bf16[8,512,128]{2,1,0:T(8,128)(2,1)S(1)}, u32[]{:S(2)}, u32[]{:S(2)}) collective-permute-start(bf16[8,512,128]{2,1,0:T(8,128)(2,1)S(1)} %all_to_all.15.near), channel_id=1, source_target_pairs={{0,1},{1,0},{2,3},{3,2},{4,5},{5,4},{6,7},{7,6},{8,9},{9,8},{10,11... | collective-permute-start | bytes 3145736 | tf_op jit(solution)/shard_map/ppermute | solution.py:135
  39.8 24.1 %copy-start.5 = (bf16[1,2048,128]{2,1,0:T(8,128)(2,1)S(1)}, bf16[1,2048,128]{2,1,0:T(8,128)(2,1)}, u32[]{:S(2)}) copy-start(bf16[1,2048,128]{2,1,0:T(8,128)(2,1)} %param.14) | copy-start | bytes 1572868
  39.8 24.1 %copy-start.7 = (bf16[1,1024,128]{2,1,0:T(8,128)(2,1)S(1)}, bf16[1,1024,128]{2,1,0:T(8,128)(2,1)}, u32[]{:S(2)}) copy-start(bf16[1,1024,128]{2,1,0:T(8,128)(2,1)} %param.12) | copy-start | bytes 786436
  39.8 42.0 %all-to-all-start = ((bf16[64,32,128]{2,1,0:T(8,128)(2,1)}), bf16[64,32,128]{2,1,0:T(8,128)(2,1)S(1)}, u32[]{:S(2)}, u32[]{:S(2)}) async-start(bf16[64,32,128]{2,1,0:T(8,128)(2,1)} %bitcast), calls=%async_computation | async-start | bytes 1048576 | tf_op jit(solution)/shard_map/all_to_all | solution.py:137
  62.6 1.3 %copy-start.6 = (bf16[1,2048,128]{2,1,0:T(8,128)(2,1)S(1)}, bf16[1,2048,128]{2,1,0:T(8,128)(2,1)}, u32[]{:S(2)}) copy-start(bf16[1,2048,128]{2,1,0:T(8,128)(2,1)} %param.15) | copy-start | bytes 1572868
  62.9 1.0 copy-start.3
  63.9 1.2 %copy-start.4 = (bf16[8,512,128]{2,1,0:T(8,128)(2,1)S(1)}, bf16[8,512,128]{2,1,0:T(8,128)(2,1)}, u32[]{:S(2)}) copy-start(bf16[8,512,128]{2,1,0:T(8,128)(2,1)} %copy-done.3) | copy-start | bytes 3145732
  81.8 35.2 %copy-start = (f32[16,32,128]{2,1,0:T(8,128)S(1)}, f32[16,32,128]{2,1,0:T(8,128)}, u32[]{:S(2)}) copy-start(f32[16,32,128]{2,1,0:T(8,128)} %master.1) | copy-start | bytes 786436
  81.8 35.2 %copy-start.1 = (f32[16,32,128]{2,1,0:T(8,128)S(1)}, f32[16,32,128]{2,1,0:T(8,128)}, u32[]{:S(2)}) copy-start(f32[16,32,128]{2,1,0:T(8,128)} %momentum.1) | copy-start | bytes 786436
  81.8 35.2 %copy-start.2 = (s32[64]{0:T(128)S(1)}, s32[64]{0:T(128)}, u32[]{:S(2)}) copy-start(s32[64]{0:T(128)} %table.1) | copy-start | bytes 772

commit v2 on v1

v2 whole, which is shorter than its diff:
```python
import jax
import jax.numpy as jnp
from jax import lax
from jax.experimental import pallas as pl
from jax.experimental.pallas import tpu as pltpu
from jax.sharding import Mesh
from jax.sharding import PartitionSpec as P

beta_first = 0.9
beta_second = 0.95
inner_rate = 0.05
decay_rate = 0.1
epsilon = 1e-08
nesterov = 0.9
outer_rate = 0.7

MIB = 1 << 20
CHUNKS = 4


def split_bf16(values):
    high = values.astype(jnp.bfloat16)
    low = (values - high.astype(jnp.float32)).astype(jnp.bfloat16)
    return high, low


def gradient_kernel(
    place, chip_held, near, far, onehot, cotangent_held, weights, sent, chip, cotangent, arrived
):
    chip_copy = pltpu.make_async_copy(chip_held, chip, arrived.at[0])
    cotangent_copy = pltpu.make_async_copy(cotangent_held, cotangent, arrived.at[1])
    chip_copy.start()
    cotangent_copy.start()
    _, pool, width = chip.shape
    stations = weights.shape[0]
    factor = (2 * stations * width) ** (-0.5)
    spot, core = place[0], place[1]
    step = 2 * core - 1
    half = pool // 2
    opposite = lax.rem(spot + stations // 2, stations)
    chip_copy.wait()
    slices = [(chip[0], spot, core), (chip[1], spot, 1 - core)]
    for held, way, first in ((near, step, core), (far, -step, 1 - core)):
        for hop in range(1, stations // 2):
            at = lax.rem(spot + hop * way + stations, stations)
            for index, side in enumerate((first, 1 - first)):
                start = (2 * (hop - 1) + index) * pool
                slices.append((held[start : start + pool], at, side))
    start = 2 * (stations // 2 - 1) * pool
    mine = [near[start + i * half : start + (i + 1) * half] for i in range(2)]
    other = [far[start + i * half : start + (i + 1) * half] for i in range(2)]
    low = core == 0
    for index, side in enumerate((core, 1 - core)):
        here, there = mine[index], other[1 - index]
        rows = jnp.concatenate(
            [jnp.where(low, here, there), jnp.where(low, there, here)], axis=0
        )
        slices.append((rows, opposite, side))
    rows = jnp.concatenate([part for part, _, _ in slices], axis=1)
    block = jnp.concatenate([weights[at, side] for _, at, side in slices], axis=0)
    product = jnp.dot(rows, block, preferred_element_type=jnp.float32) * factor
    both = jnp.concatenate(split_bf16(product), axis=1)
    taken = jnp.dot(onehot[...], both, preferred_element_type=jnp.float32)
    pre_act = taken[:, :width] + taken[:, width:]
    gate = 1.0 / (1.0 + jnp.exp(-pre_act))
    cotangent_copy.wait()
    slope = cotangent[...].astype(jnp.float32) * gate * (1.0 + pre_act * (1.0 - gate))
    slope = slope.astype(jnp.bfloat16)
    summed = lax.dot_general(
        slope, onehot[...], (((0,), (0,)), ((), ())), preferred_element_type=jnp.float32
    )
    pair = jnp.concatenate(split_bf16(summed), axis=0)
    both = jnp.dot(pair, rows, preferred_element_type=jnp.float32)
    gradient = (both[:width] + both[width:]) * factor
    signed = gradient * jnp.abs(gradient)
    for index, (_, at, side) in enumerate(slices):
        values = jnp.transpose(signed[:, index * width : (index + 1) * width])
        sent[at, side] = values.astype(jnp.bfloat16)


def module_kernel(
    table,
    early_held,
    late_held,
    master_held,
    momentum_held,
    new_master,
    new_momentum,
    first_out,
    second_out,
    totals,
    counts,
    early,
    late,
    master,
    momentum,
    arrived,
):
    paths = late.shape[0]
    modules, rows, _ = master.shape
    span = paths // CHUNKS
    pairs = []
    for chunk in range(CHUNKS):
        at = pl.ds(chunk * span, span)
        pairs.append((early_held.at[at], early.at[at]))
        pairs.append((late_held.at[at], late.at[at]))
    pairs += [(master_held, master), (momentum_held, momentum)]
    copies = [
        pltpu.make_async_copy(held, here, arrived.at[i]) for i, (held, here) in enumerate(pairs)
    ]
    for copy in copies:
        copy.start()
    totals[...] = jnp.zeros_like(totals)

    def clear(k, carry):
        counts[k] = 0
        return carry

    lax.fori_loop(0, modules, clear, 0)

    def visit(p, carry):
        module = table[p]
        counts[module] = counts[module] + 1
        signed = late[p].astype(jnp.float32)
        size = jnp.abs(signed)
        root = jnp.sqrt(size)
        gradient = jnp.where(signed < 0.0, -root, root)
        old = early[p, 0:rows].astype(jnp.float32)
        first = early[p, rows : 2 * rows].astype(jnp.float32)
        second = early[p, 2 * rows : 3 * rows].astype(jnp.float32)
        first = beta_first * first + (1.0 - beta_first) * gradient
        second = beta_second * second + (1.0 - beta_second) * size
        new = old - inner_rate * (first / (jnp.sqrt(second) + epsilon) + decay_rate * old)
        for index, values in enumerate((new, first, second)):
            totals[index, module] += values.astype(jnp.bfloat16).astype(jnp.float32)
        return carry

    for chunk in range(CHUNKS):
        copies[2 * chunk].wait()
        copies[2 * chunk + 1].wait()
        lax.fori_loop(chunk * span, (chunk + 1) * span, visit, 0, unroll=4)
    for copy in copies[2 * CHUNKS :]:
        copy.wait()

    def finish(k, carry):
        count = counts[k]
        divisor = jnp.maximum(count, 1).astype(jnp.float32)
        old = master[k]
        delta = jnp.where(count > 0, old - totals[0, k] / divisor, jnp.zeros_like(old))
        moved = nesterov * momentum[k] + delta
        new_momentum[k] = moved
        new_master[k] = old - outer_rate * (delta + nesterov * moved)
        first_out[k] = (totals[1, k] / divisor).astype(jnp.bfloat16)
        second_out[k] = (totals[2, k] / divisor).astype(jnp.bfloat16)
        return carry

    lax.fori_loop(0, modules, finish, 0)


def whole(count):
    return [pl.BlockSpec(memory_space=pltpu.VMEM) for _ in range(count)]


def in_hbm(count):
    return [pl.BlockSpec(memory_space=pltpu.HBM) for _ in range(count)]


def per_device(
    token_pool,
    batch_ids,
    module_table,
    cotangent,
    path_weights,
    first_moment,
    second_moment,
    master_weights,
    outer_momentum,
):
    stations = lax.axis_size("y")
    groups = lax.axis_size("z") * lax.axis_size("x")
    pool, width = token_pool.shape
    features = path_weights.shape[1]
    rows = features // groups
    tokens = batch_ids.shape[1]
    path_axes = ("z", "x")

    fsdp_axes = ("y", "core")
    spot, core = lax.axis_index("y"), lax.axis_index("core")

    def swap(values):
        return lax.ppermute(values, "core", [(0, 1), (1, 0)])

    def hop(values, by):
        ways = [(2 * i, 2 * ((i + by) % stations)) for i in range(stations)]
        ways += [(2 * i + 1, 2 * ((i - by) % stations) + 1) for i in range(stations)]
        return lax.ppermute(values, fsdp_axes, ways)

    packed = jnp.concatenate(
        [v[0].reshape(groups, rows, width) for v in (path_weights, first_moment, second_moment)],
        axis=1,
    )
    chip = jnp.stack([token_pool, swap(token_pool)])
    chip, packed = lax.optimization_barrier((chip, packed))
    half = pool // 2
    held = {1: hop(chip, 1), 2: hop(chip, 2)}
    held[3] = hop(held[1], 2)
    held[4] = hop(lax.dynamic_slice_in_dim(held[2], core * half, half, axis=1), 2)
    near = jnp.concatenate([held[by].reshape(-1, width) for by in sorted(held)])
    far = swap(near)

    early = lax.all_to_all(packed, path_axes, 0, 0, tiled=True)

    onehot = (
        batch_ids[0][:, None] == lax.broadcasted_iota(jnp.int32, (tokens, pool), 1)
    ).astype(jnp.bfloat16)
    place = jnp.stack([spot, core]).astype(jnp.int32)

    sent = pl.pallas_call(
        gradient_kernel,
        out_shape=jax.ShapeDtypeStruct((stations, 2, width, width), jnp.bfloat16),
        in_specs=[pl.BlockSpec(memory_space=pltpu.SMEM)]
        + in_hbm(1)
        + whole(3)
        + in_hbm(1)
        + whole(1),
        out_specs=pl.BlockSpec(memory_space=pltpu.VMEM),
        scratch_shapes=[
            pltpu.VMEM((2, pool, width), jnp.bfloat16),
            pltpu.VMEM((tokens, width), jnp.bfloat16),
            pltpu.SemaphoreType.DMA((2,)),
        ],
        compiler_params=pltpu.CompilerParams(vmem_limit_bytes=20 * MIB),
        cost_estimate=pl.CostEstimate(
            flops=2_000_000_000, bytes_accessed=5 * MIB, transcendentals=tokens * width
        ),
        name="path_gradient",
    )(place, chip, near, far, onehot, cotangent[0], path_weights[0].reshape(stations, 2, width, width))

    sent, early = lax.optimization_barrier((sent, early))
    late = lax.all_to_all(sent.reshape(groups, rows, width), path_axes, 0, 0, tiled=True)

    shape = master_weights.shape
    return pl.pallas_call(
        module_kernel,
        out_shape=(
            jax.ShapeDtypeStruct(shape, jnp.float32),
            jax.ShapeDtypeStruct(shape, jnp.float32),
            jax.ShapeDtypeStruct(shape, jnp.bfloat16),
            jax.ShapeDtypeStruct(shape, jnp.bfloat16),
        ),
        in_specs=[pl.BlockSpec(memory_space=pltpu.SMEM)] + in_hbm(4),
        out_specs=tuple(whole(4)),
        scratch_shapes=[
            pltpu.VMEM((3,) + shape, jnp.float32),
            pltpu.SMEM((shape[0],), jnp.int32),
            pltpu.VMEM((groups, 3 * rows, width), jnp.bfloat16),
            pltpu.VMEM((groups, rows, width), jnp.bfloat16),
            pltpu.VMEM(shape, jnp.float32),
            pltpu.VMEM(shape, jnp.float32),
            pltpu.SemaphoreType.DMA((2 * CHUNKS + 2,)),
        ],
        compiler_params=pltpu.CompilerParams(vmem_limit_bytes=56 * MIB),
        cost_estimate=pl.CostEstimate(
            flops=10_000_000, bytes_accessed=4 * MIB, transcendentals=4 * groups * rows * width
        ),
        name="module_update",
    )(module_table, early, late, master_weights, outer_momentum)


def solution(mesh):
    lengths = (8, 8, 8, 2)
    split = Mesh(mesh.devices.reshape(lengths), ("z", "x", "y", "core"))
    path = ("z", "x")
    fsdp = ("y", "core")
    in_specs = (
        P(None, fsdp),
        P(path, None),
        P(),
        P(path, None, fsdp),
        P(path, None, fsdp),
        P(path, None, fsdp),
        P(path, None, fsdp),
        P(None, path, fsdp),
        P(None, path, fsdp),
    )
    out_specs = (P(None, path, fsdp),) * 4
    return jax.shard_map(
        per_device, mesh=split, in_specs=in_specs, out_specs=out_specs, check_vma=False
    )
```

time: 120 us -> 101 us (0.84)
  the two profiles are of different devices: /device:TPU:6 before, /device:TPU:16 now
where the time goes in v2:
time: 101 us
  starting transfers between devices  43.8 us (43%)
  blocking collectives  26.5 us (26%)
  waiting for transfers between devices  18.5 us (18%)
  Pallas kernels  8.31 us (8%)
  other arithmetic  3.05 us (3%)
    all_to_all x1, blocking collectives, per_device(): lax.all_to_all(sent.reshape(groups, rows, width), path_axes, 0, 0, tiled=...  26.5 us
    all_to_all x1, starting transfers between devices, per_device(): early = lax.all_to_all(packed, path_axes, 0, 0, tiled=True)  22.9 us
    ppermute x4, starting transfers between devices, hop(): return lax.ppermute(values, fsdp_axes, ways)  17.1 us
    ppermute x4, waiting for transfers between devices, hop(): return lax.ppermute(values, fsdp_axes, ways)  9.45 us
    all_to_all x1, waiting for transfers between devices, per_device(): early = lax.all_to_all(packed, path_axes, 0, 0, tiled=True)  6.93 us
    pallas_call x1, Pallas kernels, per_device(): pl.pallas_call(module_kernel, out_shape=(jax.ShapeDtypeStruct(shape, jnp....  4.6 us
    ppermute x2, starting transfers between devices, swap(): return lax.ppermute(values, 'core', [(0, 1), (1, 0)])  3.84 us
    pallas_call x1, Pallas kernels, per_device(): pl.pallas_call(gradient_kernel, out_shape=jax.ShapeDtypeStruct((stations,...  3.71 us
  transfers between devices with their start and end apart: 7, of which 4 were waited for; matrix products, arithmetic and copies ran while one was open for 3% of the time, Pallas kernels for 4%

profile of v2, /device:TPU:16, one launch (start us, length us, event | category | flops | bytes accessed | tf_op | source)
XLA Modules:
  0.0 100.9 jit_solution(12079791682157263183)
XLA Ops:
  0.6 1.9 %collective-permute-start = (bf16[512,128]{1,0:T(8,128)(2,1)}, bf16[512,128]{1,0:T(8,128)(2,1)S(1)}, u32[]{:S(2)}, u32[]{:S(2)}) collective-permute-start(bf16[512,128]{1,0:T(8,128)(2,1)} %param.9), channel_id=1, source_target_pairs={{0,1},{1,0},{2,3},{3,2},{4,5},{5,4},{6,7},{7,6},{8,9},{9,8},{10,11... | collective-permute-start | bytes 393224 | tf_op jit(solution)/shard_map/ppermute | solution.py:191
  2.6 2.7 %pad_maximum_fusion = bf16[64,96,128]{2,1,0:T(8,128)(2,1)} fusion(bf16[64,32,128]{2,1,0:T(8,128)(2,1)} %bitcast.20, bf16[64,32,128]{2,1,0:T(8,128)(2,1)} %bitcast.21, bf16[64,32,128]{2,1,0:T(8,128)(2,1)} %bitcast.16), kind=kLoop, calls=%fused_computation.2 | loop fusion | flops 4718592 | bytes 3145728 | tf_op jit(solution)/shard_map/concatenate | solution.py:198
  5.2 0.0 collective-permute-done
  5.3 22.9 %all-to-all-start = ((bf16[64,96,128]{2,1,0:T(8,128)(2,1)}), bf16[64,96,128]{2,1,0:T(8,128)(2,1)}, u32[]{:S(2)}, u32[]{:S(2)}) async-start(bf16[64,96,128]{2,1,0:T(8,128)(2,1)} %pad_maximum_fusion), calls=%async_computation | async-start | bytes 3145728 | tf_op jit(solution)/shard_map/all_to_all | solution.py:211
  28.1 0.0 copy-start.3
  28.1 3.6 %collective-permute-start.1 = (bf16[2,512,128]{2,1,0:T(8,128)(2,1)S(1)}, bf16[2,512,128]{2,1,0:T(8,128)(2,1)S(1)}, u32[]{:S(2)}, u32[]{:S(2)}) collective-permute-start(bf16[2,512,128]{2,1,0:T(8,128)(2,1)S(1)} %pad_maximum_fusion.2.chip_held), channel_id=1, source_target_pairs={{0,2},{2,4},{4,6},{6,8},{8,10},{10,12},{12,14},{14,0},{1,15},{3,1}... | collective-permute-start | bytes 786440 | tf_op jit(solution)/shard_map/ppermute | solution.py:196
  31.7 5.9 %collective-permute-start.2 = (bf16[2,512,128]{2,1,0:T(8,128)(2,1)S(1)}, bf16[2,512,128]{2,1,0:T(8,128)(2,1)S(1)}, u32[]{:S(2)}, u32[]{:S(2)}) collective-permute-start(bf16[2,512,128]{2,1,0:T(8,128)(2,1)S(1)} %pad_maximum_fusion.2.chip_held), channel_id=1, source_target_pairs={{0,4},{2,6},{4,8},{6,10},{8,12},{10,14},{12,0},{14,2},{1,13},{3,15... | collective-permute-start | bytes 786440 | tf_op jit(solution)/shard_map/ppermute | solution.py:196
  37.7 0.0 collective-permute-done.1
  37.7 3.8 %collective-permute-start.3 = (bf16[2,512,128]{2,1,0:T(8,128)(2,1)S(1)}, bf16[2,512,128]{2,1,0:T(8,128)(2,1)S(1)}, u32[]{:S(2)}, u32[]{:S(2)}) collective-permute-start(bf16[2,512,128]{2,1,0:T(8,128)(2,1)S(1)} %collective-permute-done.1), channel_id=1, source_target_pairs={{0,4},{2,6},{4,8},{6,10},{8,12},{10,14},{12,0},{14,2},{1,13},{3,15... | collective-permute-start | bytes 786440 | tf_op jit(solution)/shard_map/ppermute | solution.py:196
  41.5 0.0 copy-start
  41.6 0.0 copy-start.1
  41.6 3.4 %collective-permute-done.2 = bf16[2,512,128]{2,1,0:T(8,128)(2,1)S(1)} collective-permute-done((bf16[2,512,128]{2,1,0:T(8,128)(2,1)S(1)}, bf16[2,512,128]{2,1,0:T(8,128)(2,1)S(1)}, u32[]{:S(2)}, u32[]{:S(2)}) %collective-permute-start.2) | collective-permute-done | bytes 262176 | tf_op jit(solution)/shard_map/ppermute | solution.py:196
  44.9 3.8 %collective-permute-start.4 = (bf16[2,256,128]{2,1,0:T(8,128)(2,1)S(1)}, bf16[2,256,128]{2,1,0:T(8,128)(2,1)S(1)}, u32[]{:S(2)}, u32[]{:S(2)}) collective-permute-start(bf16[2,256,128]{2,1,0:T(8,128)(2,1)S(1)} %constant_dynamic-slice_fusion), channel_id=1, source_target_pairs={{0,4},{2,6},{4,8},{6,10},{8,12},{10,14},{12,0},{14,2},{1,13},{3,15... | collective-permute-start | bytes 393224 | tf_op jit(solution)/shard_map/ppermute | solution.py:196
  48.7 6.1 %collective-permute-done.4 = bf16[2,256,128]{2,1,0:T(8,128)(2,1)S(1)} collective-permute-done((bf16[2,256,128]{2,1,0:T(8,128)(2,1)S(1)}, bf16[2,256,128]{2,1,0:T(8,128)(2,1)S(1)}, u32[]{:S(2)}, u32[]{:S(2)}) %collective-permute-start.4) | collective-permute-done | bytes 131104 | tf_op jit(solution)/shard_map/ppermute | solution.py:196
  54.8 0.0 collective-permute-done.3
  54.8 0.1 pad_maximum_fusion.1.near
  54.9 1.9 %collective-permute-start.5 = (bf16[3584,128]{1,0:T(8,128)(2,1)S(1)}, bf16[3584,128]{1,0:T(8,128)(2,1)S(1)}, u32[]{:S(2)}, u32[]{:S(2)}) collective-permute-start(bf16[3584,128]{1,0:T(8,128)(2,1)S(1)} %pad_maximum_fusion.1.near), channel_id=1, source_target_pairs={{0,1},{1,0},{2,3},{3,2},{4,5},{5,4},{6,7},{7,6},{8,9},{9,8},{10,11... | collective-permute-start | bytes 2752520 | tf_op jit(solution)/shard_map/ppermute | solution.py:191
  56.8 0.1 pad_add_fusion.place
  56.9 0.2 fusion.onehot
  57.1 2.1 %collective-permute-done.5.far = bf16[3584,128]{1,0:T(8,128)(2,1)S(1)} collective-permute-done((bf16[3584,128]{1,0:T(8,128)(2,1)S(1)}, bf16[3584,128]{1,0:T(8,128)(2,1)S(1)}, u32[]{:S(2)}, u32[]{:S(2)}) %collective-permute-start.5) | collective-permute-done | bytes 917536 | tf_op jit(solution)/shard_map/ppermute | solution.py:191
  59.2 3.7 %path_gradient.1 = bf16[8,2,128,128]{3,2,1,0:T(8,128)(2,1)S(1)} custom-call(s32[2]{0:T(128)S(1)} %pad_add_fusion.place, bf16[2,512,128]{2,1,0:T(8,128)(2,1)S(1)} %pad_maximum_fusion.2.chip_held, bf16[3584,128]{1,0:T(8,128)(2,1)S(1)} %pad_maximum_fusion.1.near, bf16[3584,128]{1,0:T(8,128)(2,1)S(1)} %collective-permute-done.5.far, ...), custom_call_target="tpu_custom_call" | custom-call | flops 2000000000 | bytes 5242880 | tf_op jit(solution)/shard_map/path_gradient/pallas_call | solution.py:218
  62.9 6.9 %all-to-all-done.early_held = bf16[64,96,128]{2,1,0:T(8,128)(2,1)} async-done(((bf16[64,96,128]{2,1,0:T(8,128)(2,1)}), bf16[64,96,128]{2,1,0:T(8,128)(2,1)}, u32[]{:S(2)}, u32[]{:S(2)}) %all-to-all-start) | async-done | bytes 1572896 | tf_op jit(solution)/shard_map/all_to_all | solution.py:211
  69.9 26.5 %all_to_all.10.late_held = bf16[64,32,128]{2,1,0:T(8,128)(2,1)} all-to-all(bf16[64,32,128]{2,1,0:T(8,128)(2,1)S(1)} %bitcast.15), channel_id=1, replica_groups=mesh['z'=8,'x'=8,'y'=8,'core'=2] {'z','x'}, dimensions={0} | all-to-all | bytes 1048576 | tf_op jit(solution)/shard_map/all_to_all | solution.py:240
  96.3 4.6 %module_update.1 = (f32[16,32,128]{2,1,0:T(8,128)}, f32[16,32,128]{2,1,0:T(8,128)}, bf16[16,32,128]{2,1,0:T(8,128)(2,1)}, bf16[16,32,128]{2,1,0:T(8,128)(2,1)}) custom-call(s32[64]{0:T(128)} %table.1, bf16[64,96,128]{2,1,0:T(8,128)(2,1)} %all-to-all-done.early_held, bf16[64,32,128]{2,1,0:T(8,128)(2,1)} %all_to_all.10.late_held, f32[16,32,128]{2,1,0:T(8,128)} %master_held.1, ...), custom_call_target="tpu_custom_call" | custom-call | flops 10000000 | bytes 4194304 | tf_op jit(solution)/shard_map/module_update/pallas_call | solution.py:243
  (7 shorter events, 0.0 us)
Async XLA Ops:
  0.6 4.6 %collective-permute-start = (bf16[512,128]{1,0:T(8,128)(2,1)}, bf16[512,128]{1,0:T(8,128)(2,1)S(1)}, u32[]{:S(2)}, u32[]{:S(2)}) collective-permute-start(bf16[512,128]{1,0:T(8,128)(2,1)} %param.9), channel_id=1, source_target_pairs={{0,1},{1,0},{2,3},{3,2},{4,5},{5,4},{6,7},{7,6},{8,9},{9,8},{10,11... | collective-permute-start | bytes 393224 | tf_op jit(solution)/shard_map/ppermute | solution.py:191
  2.6 2.7 %copy-start.2 = (bf16[512,128]{1,0:T(8,128)(2,1)S(1)}, bf16[512,128]{1,0:T(8,128)(2,1)}, u32[]{:S(2)}) copy-start(bf16[512,128]{1,0:T(8,128)(2,1)} %param.9) | copy-start | bytes 393220
  5.3 64.6 %all-to-all-start = ((bf16[64,96,128]{2,1,0:T(8,128)(2,1)}), bf16[64,96,128]{2,1,0:T(8,128)(2,1)}, u32[]{:S(2)}, u32[]{:S(2)}) async-start(bf16[64,96,128]{2,1,0:T(8,128)(2,1)} %pad_maximum_fusion), calls=%async_computation | async-start | bytes 3145728 | tf_op jit(solution)/shard_map/all_to_all | solution.py:211
  28.1 28.7 %copy-start.3 = (s32[1,1024]{1,0:T(1,128)S(1)}, s32[1,1024]{1,0:T(1,128)}, u32[]{:S(2)}) copy-start(s32[1,1024]{1,0:T(1,128)} %param.10) | copy-start | bytes 12292
  28.1 9.6 %collective-permute-start.1 = (bf16[2,512,128]{2,1,0:T(8,128)(2,1)S(1)}, bf16[2,512,128]{2,1,0:T(8,128)(2,1)S(1)}, u32[]{:S(2)}, u32[]{:S(2)}) collective-permute-start(bf16[2,512,128]{2,1,0:T(8,128)(2,1)S(1)} %pad_maximum_fusion.2.chip_held), channel_id=1, source_target_pairs={{0,2},{2,4},{4,6},{6,8},{8,10},{10,12},{12,14},{14,0},{1,15},{3,1}... | collective-permute-start | bytes 786440 | tf_op jit(solution)/shard_map/ppermute | solution.py:196
  31.7 13.2 %collective-permute-start.2 = (bf16[2,512,128]{2,1,0:T(8,128)(2,1)S(1)}, bf16[2,512,128]{2,1,0:T(8,128)(2,1)S(1)}, u32[]{:S(2)}, u32[]{:S(2)}) collective-permute-start(bf16[2,512,128]{2,1,0:T(8,128)(2,1)S(1)} %pad_maximum_fusion.2.chip_held), channel_id=1, source_target_pairs={{0,4},{2,6},{4,8},{6,10},{8,12},{10,14},{12,0},{14,2},{1,13},{3,15... | collective-permute-start | bytes 786440 | tf_op jit(solution)/shard_map/ppermute | solution.py:196
  37.7 17.1 %collective-permute-start.3 = (bf16[2,512,128]{2,1,0:T(8,128)(2,1)S(1)}, bf16[2,512,128]{2,1,0:T(8,128)(2,1)S(1)}, u32[]{:S(2)}, u32[]{:S(2)}) collective-permute-start(bf16[2,512,128]{2,1,0:T(8,128)(2,1)S(1)} %collective-permute-done.1), channel_id=1, source_target_pairs={{0,4},{2,6},{4,8},{6,10},{8,12},{10,14},{12,0},{14,2},{1,13},{3,15... | collective-permute-start | bytes 786440 | tf_op jit(solution)/shard_map/ppermute | solution.py:196
  41.5 17.7 %copy-start = (bf16[1,2048,128]{2,1,0:T(8,128)(2,1)S(1)}, bf16[1,2048,128]{2,1,0:T(8,128)(2,1)}, u32[]{:S(2)}) copy-start(bf16[1,2048,128]{2,1,0:T(8,128)(2,1)} %param.13) | copy-start | bytes 1572868
  41.6 17.7 %copy-start.1 = (bf16[1,1024,128]{2,1,0:T(8,128)(2,1)S(1)}, bf16[1,1024,128]{2,1,0:T(8,128)(2,1)}, u32[]{:S(2)}) copy-start(bf16[1,1024,128]{2,1,0:T(8,128)(2,1)} %param.12) | copy-start | bytes 786436
  44.9 9.9 %collective-permute-start.4 = (bf16[2,256,128]{2,1,0:T(8,128)(2,1)S(1)}, bf16[2,256,128]{2,1,0:T(8,128)(2,1)S(1)}, u32[]{:S(2)}, u32[]{:S(2)}) collective-permute-start(bf16[2,256,128]{2,1,0:T(8,128)(2,1)S(1)} %constant_dynamic-slice_fusion), channel_id=1, source_target_pairs={{0,4},{2,6},{4,8},{6,10},{8,12},{10,14},{12,0},{14,2},{1,13},{3,15... | collective-permute-start | bytes 393224 | tf_op jit(solution)/shard_map/ppermute | solution.py:196
  54.9 4.4 %collective-permute-start.5 = (bf16[3584,128]{1,0:T(8,128)(2,1)S(1)}, bf16[3584,128]{1,0:T(8,128)(2,1)S(1)}, u32[]{:S(2)}, u32[]{:S(2)}) collective-permute-start(bf16[3584,128]{1,0:T(8,128)(2,1)S(1)} %pad_maximum_fusion.1.near), channel_id=1, source_target_pairs={{0,1},{1,0},{2,3},{3,2},{4,5},{5,4},{6,7},{7,6},{8,9},{9,8},{10,11... | collective-permute-start | bytes 2752520 | tf_op jit(solution)/shard_map/ppermute | solution.py:191

commit v3 on v2

--- a/solution.py
+++ b/solution.py
@@ -16,12 +16,41 @@
 
 MIB = 1 << 20
 CHUNKS = 4
+TINY = 1e-36
 
 
 def split_bf16(values):
     high = values.astype(jnp.bfloat16)
     low = (values - high.astype(jnp.float32)).astype(jnp.bfloat16)
     return high, low
+
+
+def pack_kernel(weights, first, second, packed, held, arrived, left):
+    groups, rows, _ = weights.shape
+    span = groups // CHUNKS
+    parts = [pl.ds(chunk * span, span) for chunk in range(CHUNKS)]
+    inward = [
+        [
+            pltpu.make_async_copy(
+                part.at[at], held.at[at, pl.ds(i * rows, rows)], arrived.at[chunk, i]
+            )
+            for i, part in enumerate((weights, first, second))
+        ]
+        for chunk, at in enumerate(parts)
+    ]
+    outward = [
+        pltpu.make_async_copy(held.at[at], packed.at[at], left.at[chunk])
+        for chunk, at in enumerate(parts)
+    ]
+    for copies in inward:
+        for copy in copies:
+            copy.start()
+    for copies, away in zip(inward, outward):
+        for copy in copies:
+            copy.wait()
+        away.start()
+    for away in outward:
+        away.wait()
 
 
 def gradient_kernel(
@@ -123,14 +152,14 @@
         counts[module] = counts[module] + 1
         signed = late[p].astype(jnp.float32)
         size = jnp.abs(signed)
-        root = jnp.sqrt(size)
-        gradient = jnp.where(signed < 0.0, -root, root)
+        gradient = signed * lax.rsqrt(jnp.maximum(size, TINY))
         old = early[p, 0:rows].astype(jnp.float32)
         first = early[p, rows : 2 * rows].astype(jnp.float32)
         second = early[p, 2 * rows : 3 * rows].astype(jnp.float32)
         first = beta_first * first + (1.0 - beta_first) * gradient
         second = beta_second * second + (1.0 - beta_second) * size
-        new = old - inner_rate * (first / (jnp.sqrt(second) + epsilon) + decay_rate * old)
+        root = second * lax.rsqrt(second)
+        new = old - inner_rate * (first / (root + epsilon) + decay_rate * old)
         for index, values in enumerate((new, first, second)):
             totals[index, module] += values.astype(jnp.bfloat16).astype(jnp.float32)
         return carry
@@ -138,7 +167,7 @@
     for chunk in range(CHUNKS):
         copies[2 * chunk].wait()
         copies[2 * chunk + 1].wait()
-        lax.fori_loop(chunk * span, (chunk + 1) * span, visit, 0, unroll=4)
+        lax.fori_loop(chunk * span, (chunk + 1) * span, visit, 0, unroll=8)
     for copy in copies[2 * CHUNKS :]:
         copy.wait()
 
@@ -154,7 +183,7 @@
         second_out[k] = (totals[2, k] / divisor).astype(jnp.bfloat16)
         return carry
 
-    lax.fori_loop(0, modules, finish, 0)
+    lax.fori_loop(0, modules, finish, 0, unroll=4)
 
 
 def whole(count):
@@ -195,10 +224,21 @@
         ways += [(2 * i + 1, 2 * ((i - by) % stations) + 1) for i in range(stations)]
         return lax.ppermute(values, fsdp_axes, ways)
 
-    packed = jnp.concatenate(
-        [v[0].reshape(groups, rows, width) for v in (path_weights, first_moment, second_moment)],
-        axis=1,
-    )
+    packed = pl.pallas_call(
+        pack_kernel,
+        out_shape=jax.ShapeDtypeStruct((groups, 3 * rows, width), jnp.bfloat16),
+        in_specs=in_hbm(3),
+        out_specs=pl.BlockSpec(memory_space=pltpu.HBM),
+        scratch_shapes=[
+            pltpu.VMEM((groups, 3 * rows, width), jnp.bfloat16),
+            pltpu.SemaphoreType.DMA((CHUNKS, 3)),
+            pltpu.SemaphoreType.DMA((CHUNKS,)),
+        ],
+        compiler_params=pltpu.CompilerParams(vmem_limit_bytes=56 * MIB),
+        cost_estimate=pl.CostEstimate(flops=0, bytes_accessed=3 * MIB, transcendentals=0),
+        name="pack",
+    )(*[v[0].reshape(groups, rows, width) for v in (path_weights, first_moment, second_moment)])
+
     chip = jnp.stack([token_pool, swap(token_pool)])
     chip, packed = lax.optimization_barrier((chip, packed))
     half = pool // 2

time: 101 us -> 101 us (level)
  other arithmetic: 3.05 us -> 0.4 us
  Pallas kernels: 8.31 us -> 10 us
    concatenate x1 -> x0, other arithmetic: 2.65 us -> none  [per_device(): jnp.concatenate([v[0].reshape(groups, rows, width) for v in (path_weights...]
    pallas_call x0 -> x1, Pallas kernels: none -> 2.41 us  [per_device(): pl.pallas_call(pack_kernel, out_shape=jax.ShapeDtypeStruct((groups, 3 * r...]
  transfers between devices with their start and end apart: 7 -> 7, of which waited for: 4 -> 4; matrix products, arithmetic and copies ran while one was open for 3% -> 0% of each run, Pallas kernels for 4% -> 6%
where the time goes in v3:
time: 101 us; the launch traced here: 100 us
  starting transfers between devices  43.8 us (43%)
  blocking collectives  26.5 us (26%)
  waiting for transfers between devices  18.5 us (18%)
  Pallas kernels  10 us (10%)
    all_to_all x1, blocking collectives, per_device(): lax.all_to_all(sent.reshape(groups, rows, width), path_axes, 0, 0, tiled=...  26.5 us
    all_to_all x1, starting transfers between devices, per_device(): early = lax.all_to_all(packed, path_axes, 0, 0, tiled=True)  22.9 us
    ppermute x4, starting transfers between devices, hop(): return lax.ppermute(values, fsdp_axes, ways)  17.1 us
    ppermute x4, waiting for transfers between devices, hop(): return lax.ppermute(values, fsdp_axes, ways)  9.45 us
    all_to_all x1, waiting for transfers between devices, per_device(): early = lax.all_to_all(packed, path_axes, 0, 0, tiled=True)  6.93 us
    pallas_call x1, Pallas kernels, per_device(): pl.pallas_call(module_kernel, out_shape=(jax.ShapeDtypeStruct(shape, jnp....  3.93 us
    ppermute x2, starting transfers between devices, swap(): return lax.ppermute(values, 'core', [(0, 1), (1, 0)])  3.84 us
    pallas_call x1, Pallas kernels, per_device(): pl.pallas_call(gradient_kernel, out_shape=jax.ShapeDtypeStruct((stations,...  3.71 us
  transfers between devices with their start and end apart: 7, of which 4 were waited for; matrix products, arithmetic and copies ran while one was open for 0% of the time, Pallas kernels for 6%

profile of v3, /device:TPU:16, one launch (start us, length us, event | category | flops | bytes accessed | tf_op | source)
XLA Modules:
  0.0 100.0 jit_solution(10544536533540326368)
XLA Ops:
  0.6 1.9 %collective-permute-start = (bf16[512,128]{1,0:T(8,128)(2,1)}, bf16[512,128]{1,0:T(8,128)(2,1)S(1)}, u32[]{:S(2)}, u32[]{:S(2)}) collective-permute-start(bf16[512,128]{1,0:T(8,128)(2,1)} %param.9), channel_id=1, source_target_pairs={{0,1},{1,0},{2,3},{3,2},{4,5},{5,4},{6,7},{7,6},{8,9},{9,8},{10,11... | collective-permute-start | bytes 393224 | tf_op jit(solution)/shard_map/ppermute | solution.py:220
  2.6 2.4 %pack.1 = bf16[64,96,128]{2,1,0:T(8,128)(2,1)} custom-call(bf16[64,32,128]{2,1,0:T(8,128)(2,1)} %bitcast.16, bf16[64,32,128]{2,1,0:T(8,128)(2,1)} %bitcast.20, bf16[64,32,128]{2,1,0:T(8,128)(2,1)} %bitcast.21), custom_call_target="tpu_custom_call" | custom-call | bytes 3145728 | tf_op jit(solution)/shard_map/pack/pallas_call | solution.py:227
  5.0 0.0 collective-permute-done
  5.0 22.9 %all-to-all-start = ((bf16[64,96,128]{2,1,0:T(8,128)(2,1)}), bf16[64,96,128]{2,1,0:T(8,128)(2,1)}, u32[]{:S(2)}, u32[]{:S(2)}) async-start(bf16[64,96,128]{2,1,0:T(8,128)(2,1)} %pack.1), calls=%async_computation | async-start | bytes 3145728 | tf_op jit(solution)/shard_map/all_to_all | solution.py:251
  27.9 0.0 copy-start.3
  27.9 3.6 %collective-permute-start.1 = (bf16[2,512,128]{2,1,0:T(8,128)(2,1)S(1)}, bf16[2,512,128]{2,1,0:T(8,128)(2,1)S(1)}, u32[]{:S(2)}, u32[]{:S(2)}) collective-permute-start(bf16[2,512,128]{2,1,0:T(8,128)(2,1)S(1)} %pad_maximum_fusion.1.chip_held), channel_id=1, source_target_pairs={{0,2},{2,4},{4,6},{6,8},{8,10},{10,12},{12,14},{14,0},{1,15},{3,1}... | collective-permute-start | bytes 786440 | tf_op jit(solution)/shard_map/ppermute | solution.py:225
  31.5 5.9 %collective-permute-start.2 = (bf16[2,512,128]{2,1,0:T(8,128)(2,1)S(1)}, bf16[2,512,128]{2,1,0:T(8,128)(2,1)S(1)}, u32[]{:S(2)}, u32[]{:S(2)}) collective-permute-start(bf16[2,512,128]{2,1,0:T(8,128)(2,1)S(1)} %pad_maximum_fusion.1.chip_held), channel_id=1, source_target_pairs={{0,4},{2,6},{4,8},{6,10},{8,12},{10,14},{12,0},{14,2},{1,13},{3,15... | collective-permute-start | bytes 786440 | tf_op jit(solution)/shard_map/ppermute | solution.py:225
  37.5 0.0 collective-permute-done.1
  37.5 3.8 %collective-permute-start.3 = (bf16[2,512,128]{2,1,0:T(8,128)(2,1)S(1)}, bf16[2,512,128]{2,1,0:T(8,128)(2,1)S(1)}, u32[]{:S(2)}, u32[]{:S(2)}) collective-permute-start(bf16[2,512,128]{2,1,0:T(8,128)(2,1)S(1)} %collective-permute-done.1), channel_id=1, source_target_pairs={{0,4},{2,6},{4,8},{6,10},{8,12},{10,14},{12,0},{14,2},{1,13},{3,15... | collective-permute-start | bytes 786440 | tf_op jit(solution)/shard_map/ppermute | solution.py:225
  41.3 0.0 copy-start
  41.3 0.0 copy-start.1
  41.3 3.4 %collective-permute-done.2 = bf16[2,512,128]{2,1,0:T(8,128)(2,1)S(1)} collective-permute-done((bf16[2,512,128]{2,1,0:T(8,128)(2,1)S(1)}, bf16[2,512,128]{2,1,0:T(8,128)(2,1)S(1)}, u32[]{:S(2)}, u32[]{:S(2)}) %collective-permute-start.2) | collective-permute-done | bytes 262176 | tf_op jit(solution)/shard_map/ppermute | solution.py:225
  44.7 3.8 %collective-permute-start.4 = (bf16[2,256,128]{2,1,0:T(8,128)(2,1)S(1)}, bf16[2,256,128]{2,1,0:T(8,128)(2,1)S(1)}, u32[]{:S(2)}, u32[]{:S(2)}) collective-permute-start(bf16[2,256,128]{2,1,0:T(8,128)(2,1)S(1)} %constant_dynamic-slice_fusion), channel_id=1, source_target_pairs={{0,4},{2,6},{4,8},{6,10},{8,12},{10,14},{12,0},{14,2},{1,13},{3,15... | collective-permute-start | bytes 393224 | tf_op jit(solution)/shard_map/ppermute | solution.py:225
  48.5 6.1 %collective-permute-done.4 = bf16[2,256,128]{2,1,0:T(8,128)(2,1)S(1)} collective-permute-done((bf16[2,256,128]{2,1,0:T(8,128)(2,1)S(1)}, bf16[2,256,128]{2,1,0:T(8,128)(2,1)S(1)}, u32[]{:S(2)}, u32[]{:S(2)}) %collective-permute-start.4) | collective-permute-done | bytes 131104 | tf_op jit(solution)/shard_map/ppermute | solution.py:225
  54.6 0.0 collective-permute-done.3
  54.6 0.1 pad_maximum_fusion.near
  54.6 1.9 %collective-permute-start.5 = (bf16[3584,128]{1,0:T(8,128)(2,1)S(1)}, bf16[3584,128]{1,0:T(8,128)(2,1)S(1)}, u32[]{:S(2)}, u32[]{:S(2)}) collective-permute-start(bf16[3584,128]{1,0:T(8,128)(2,1)S(1)} %pad_maximum_fusion.near), channel_id=1, source_target_pairs={{0,1},{1,0},{2,3},{3,2},{4,5},{5,4},{6,7},{7,6},{8,9},{9,8},{10,11... | collective-permute-start | bytes 2752520 | tf_op jit(solution)/shard_map/ppermute | solution.py:220
  56.6 0.1 pad_add_fusion.place
  56.7 0.2 fusion.onehot
  56.9 2.1 %collective-permute-done.5.far = bf16[3584,128]{1,0:T(8,128)(2,1)S(1)} collective-permute-done((bf16[3584,128]{1,0:T(8,128)(2,1)S(1)}, bf16[3584,128]{1,0:T(8,128)(2,1)S(1)}, u32[]{:S(2)}, u32[]{:S(2)}) %collective-permute-start.5) | collective-permute-done | bytes 917536 | tf_op jit(solution)/shard_map/ppermute | solution.py:220
  59.0 3.7 %path_gradient.1 = bf16[8,2,128,128]{3,2,1,0:T(8,128)(2,1)S(1)} custom-call(s32[2]{0:T(128)S(1)} %pad_add_fusion.place, bf16[2,512,128]{2,1,0:T(8,128)(2,1)S(1)} %pad_maximum_fusion.1.chip_held, bf16[3584,128]{1,0:T(8,128)(2,1)S(1)} %pad_maximum_fusion.near, bf16[3584,128]{1,0:T(8,128)(2,1)S(1)} %collective-permute-done.5.far, ...), custom_call_target="tpu_custom_call" | custom-call | flops 2000000000 | bytes 5242880 | tf_op jit(solution)/shard_map/path_gradient/pallas_call | solution.py:258
  62.7 6.9 %all-to-all-done.early_held = bf16[64,96,128]{2,1,0:T(8,128)(2,1)} async-done(((bf16[64,96,128]{2,1,0:T(8,128)(2,1)}), bf16[64,96,128]{2,1,0:T(8,128)(2,1)}, u32[]{:S(2)}, u32[]{:S(2)}) %all-to-all-start) | async-done | bytes 1572896 | tf_op jit(solution)/shard_map/all_to_all | solution.py:251
  69.7 26.5 %all_to_all.10.late_held = bf16[64,32,128]{2,1,0:T(8,128)(2,1)} all-to-all(bf16[64,32,128]{2,1,0:T(8,128)(2,1)S(1)} %bitcast.15), channel_id=1, replica_groups=mesh['z'=8,'x'=8,'y'=8,'core'=2] {'z','x'}, dimensions={0} | all-to-all | bytes 1048576 | tf_op jit(solution)/shard_map/all_to_all | solution.py:280
  96.1 3.9 %module_update.1 = (f32[16,32,128]{2,1,0:T(8,128)}, f32[16,32,128]{2,1,0:T(8,128)}, bf16[16,32,128]{2,1,0:T(8,128)(2,1)}, bf16[16,32,128]{2,1,0:T(8,128)(2,1)}) custom-call(s32[64]{0:T(128)} %table.1, bf16[64,96,128]{2,1,0:T(8,128)(2,1)} %all-to-all-done.early_held, bf16[64,32,128]{2,1,0:T(8,128)(2,1)} %all_to_all.10.late_held, f32[16,32,128]{2,1,0:T(8,128)} %master_held.1, ...), custom_call_target="tpu_custom_call" | custom-call | flops 10000000 | bytes 4194304 | tf_op jit(solution)/shard_map/module_update/pallas_call | solution.py:283
  (7 shorter events, 0.0 us)
Async XLA Ops:
  0.6 4.4 %collective-permute-start = (bf16[512,128]{1,0:T(8,128)(2,1)}, bf16[512,128]{1,0:T(8,128)(2,1)S(1)}, u32[]{:S(2)}, u32[]{:S(2)}) collective-permute-start(bf16[512,128]{1,0:T(8,128)(2,1)} %param.9), channel_id=1, source_target_pairs={{0,1},{1,0},{2,3},{3,2},{4,5},{5,4},{6,7},{7,6},{8,9},{9,8},{10,11... | collective-permute-start | bytes 393224 | tf_op jit(solution)/shard_map/ppermute | solution.py:220
  2.6 2.4 %copy-start.2 = (bf16[512,128]{1,0:T(8,128)(2,1)S(1)}, bf16[512,128]{1,0:T(8,128)(2,1)}, u32[]{:S(2)}) copy-start(bf16[512,128]{1,0:T(8,128)(2,1)} %param.9) | copy-start | bytes 393220
  5.0 64.6 %all-to-all-start = ((bf16[64,96,128]{2,1,0:T(8,128)(2,1)}), bf16[64,96,128]{2,1,0:T(8,128)(2,1)}, u32[]{:S(2)}, u32[]{:S(2)}) async-start(bf16[64,96,128]{2,1,0:T(8,128)(2,1)} %pack.1), calls=%async_computation | async-start | bytes 3145728 | tf_op jit(solution)/shard_map/all_to_all | solution.py:251
  27.9 28.7 %copy-start.3 = (s32[1,1024]{1,0:T(1,128)S(1)}, s32[1,1024]{1,0:T(1,128)}, u32[]{:S(2)}) copy-start(s32[1,1024]{1,0:T(1,128)} %param.10) | copy-start | bytes 12292
  27.9 9.6 %collective-permute-start.1 = (bf16[2,512,128]{2,1,0:T(8,128)(2,1)S(1)}, bf16[2,512,128]{2,1,0:T(8,128)(2,1)S(1)}, u32[]{:S(2)}, u32[]{:S(2)}) collective-permute-start(bf16[2,512,128]{2,1,0:T(8,128)(2,1)S(1)} %pad_maximum_fusion.1.chip_held), channel_id=1, source_target_pairs={{0,2},{2,4},{4,6},{6,8},{8,10},{10,12},{12,14},{14,0},{1,15},{3,1}... | collective-permute-start | bytes 786440 | tf_op jit(solution)/shard_map/ppermute | solution.py:225
  31.5 13.2 %collective-permute-start.2 = (bf16[2,512,128]{2,1,0:T(8,128)(2,1)S(1)}, bf16[2,512,128]{2,1,0:T(8,128)(2,1)S(1)}, u32[]{:S(2)}, u32[]{:S(2)}) collective-permute-start(bf16[2,512,128]{2,1,0:T(8,128)(2,1)S(1)} %pad_maximum_fusion.1.chip_held), channel_id=1, source_target_pairs={{0,4},{2,6},{4,8},{6,10},{8,12},{10,14},{12,0},{14,2},{1,13},{3,15... | collective-permute-start | bytes 786440 | tf_op jit(solution)/shard_map/ppermute | solution.py:225
  37.5 17.1 %collective-permute-start.3 = (bf16[2,512,128]{2,1,0:T(8,128)(2,1)S(1)}, bf16[2,512,128]{2,1,0:T(8,128)(2,1)S(1)}, u32[]{:S(2)}, u32[]{:S(2)}) collective-permute-start(bf16[2,512,128]{2,1,0:T(8,128)(2,1)S(1)} %collective-permute-done.1), channel_id=1, source_target_pairs={{0,4},{2,6},{4,8},{6,10},{8,12},{10,14},{12,0},{14,2},{1,13},{3,15... | collective-permute-start | bytes 786440 | tf_op jit(solution)/shard_map/ppermute | solution.py:225
  41.3 17.7 %copy-start = (bf16[1,2048,128]{2,1,0:T(8,128)(2,1)S(1)}, bf16[1,2048,128]{2,1,0:T(8,128)(2,1)}, u32[]{:S(2)}) copy-start(bf16[1,2048,128]{2,1,0:T(8,128)(2,1)} %param.13) | copy-start | bytes 1572868
  41.3 17.7 %copy-start.1 = (bf16[1,1024,128]{2,1,0:T(8,128)(2,1)S(1)}, bf16[1,1024,128]{2,1,0:T(8,128)(2,1)}, u32[]{:S(2)}) copy-start(bf16[1,1024,128]{2,1,0:T(8,128)(2,1)} %param.12) | copy-start | bytes 786436
  44.7 9.9 %collective-permute-start.4 = (bf16[2,256,128]{2,1,0:T(8,128)(2,1)S(1)}, bf16[2,256,128]{2,1,0:T(8,128)(2,1)S(1)}, u32[]{:S(2)}, u32[]{:S(2)}) collective-permute-start(bf16[2,256,128]{2,1,0:T(8,128)(2,1)S(1)} %constant_dynamic-slice_fusion), channel_id=1, source_target_pairs={{0,4},{2,6},{4,8},{6,10},{8,12},{10,14},{12,0},{14,2},{1,13},{3,15... | collective-permute-start | bytes 393224 | tf_op jit(solution)/shard_map/ppermute | solution.py:225
  54.6 4.4 %collective-permute-start.5 = (bf16[3584,128]{1,0:T(8,128)(2,1)S(1)}, bf16[3584,128]{1,0:T(8,128)(2,1)S(1)}, u32[]{:S(2)}, u32[]{:S(2)}) collective-permute-start(bf16[3584,128]{1,0:T(8,128)(2,1)S(1)} %pad_maximum_fusion.near), channel_id=1, source_target_pairs={{0,1},{1,0},{2,3},{3,2},{4,5},{5,4},{6,7},{7,6},{8,9},{9,8},{10,11... | collective-permute-start | bytes 2752520 | tf_op jit(solution)/shard_map/ppermute | solution.py:220

commit v4 on v3

--- a/solution.py
+++ b/solution.py
@@ -15,7 +15,7 @@
 outer_rate = 0.7
 
 MIB = 1 << 20
-CHUNKS = 4
+CHUNKS = 8
 TINY = 1e-36
 
 
@@ -53,13 +53,7 @@
         away.wait()
 
 
-def gradient_kernel(
-    place, chip_held, near, far, onehot, cotangent_held, weights, sent, chip, cotangent, arrived
-):
-    chip_copy = pltpu.make_async_copy(chip_held, chip, arrived.at[0])
-    cotangent_copy = pltpu.make_async_copy(cotangent_held, cotangent, arrived.at[1])
-    chip_copy.start()
-    cotangent_copy.start()
+def gradient_kernel(place, chip, near, far, onehot, cotangent, weights, sent):
     _, pool, width = chip.shape
     stations = weights.shape[0]
     factor = (2 * stations * width) ** (-0.5)
@@ -67,7 +61,6 @@
     step = 2 * core - 1
     half = pool // 2
     opposite = lax.rem(spot + stations // 2, stations)
-    chip_copy.wait()
     slices = [(chip[0], spot, core), (chip[1], spot, 1 - core)]
     for held, way, first in ((near, step, core), (far, -step, 1 - core)):
         for hop in range(1, stations // 2):
@@ -92,7 +85,6 @@
     taken = jnp.dot(onehot[...], both, preferred_element_type=jnp.float32)
     pre_act = taken[:, :width] + taken[:, width:]
     gate = 1.0 / (1.0 + jnp.exp(-pre_act))
-    cotangent_copy.wait()
     slope = cotangent[...].astype(jnp.float32) * gate * (1.0 + pre_act * (1.0 - gate))
     slope = slope.astype(jnp.bfloat16)
     summed = lax.dot_general(
@@ -240,7 +232,6 @@
     )(*[v[0].reshape(groups, rows, width) for v in (path_weights, first_moment, second_moment)])
 
     chip = jnp.stack([token_pool, swap(token_pool)])
-    chip, packed = lax.optimization_barrier((chip, packed))
     half = pool // 2
     held = {1: hop(chip, 1), 2: hop(chip, 2)}
     held[3] = hop(held[1], 2)
@@ -258,17 +249,8 @@
     sent = pl.pallas_call(
         gradient_kernel,
         out_shape=jax.ShapeDtypeStruct((stations, 2, width, width), jnp.bfloat16),
-        in_specs=[pl.BlockSpec(memory_space=pltpu.SMEM)]
-        + in_hbm(1)
-        + whole(3)
-        + in_hbm(1)
-        + whole(1),
+        in_specs=[pl.BlockSpec(memory_space=pltpu.SMEM)] + whole(6),
         out_specs=pl.BlockSpec(memory_space=pltpu.VMEM),
-        scratch_shapes=[
-            pltpu.VMEM((2, pool, width), jnp.bfloat16),
-            pltpu.VMEM((tokens, width), jnp.bfloat16),
-            pltpu.SemaphoreType.DMA((2,)),
-        ],
         compiler_params=pltpu.CompilerParams(vmem_limit_bytes=20 * MIB),
         cost_estimate=pl.CostEstimate(
             flops=2_000_000_000, bytes_accessed=5 * MIB, transcendentals=tokens * width

time: 101 us -> 101 us (level)
  blocking collectives: 26.5 us -> 29.2 us
  waiting for transfers between devices: 18.5 us -> 16.1 us
    all_to_all x1, waiting for transfers between devices: 6.93 us -> 3.24 us  [per_device(): early = lax.all_to_all(packed, path_axes, 0, 0, tiled=True)]
    all_to_all x1, blocking collectives: 26.5 us -> 29.2 us  [per_device(): lax.all_to_all(sent.reshape(groups, rows, width), path_axes, 0, 0, tiled=...]
    ppermute x2, waiting for transfers between devices: 2.12 us -> 3.43 us  [swap(): return lax.ppermute(values, 'core', [(0, 1), (1, 0)])]
  transfers between devices with their start and end apart: 7 -> 7, of which waited for: 4 -> 5; matrix products, arithmetic and copies ran while one was open for 0% -> 0% of each run, Pallas kernels for 6% -> 3%
where the time goes in v4:
time: 101 us; the launch traced here: 100 us
  starting transfers between devices  44 us (44%)
  blocking collectives  29.2 us (29%)
  waiting for transfers between devices  16.1 us (16%)
  Pallas kernels  9.83 us (10%)
    all_to_all x1, blocking collectives, per_device(): lax.all_to_all(sent.reshape(groups, rows, width), path_axes, 0, 0, tiled=...  29.2 us
    all_to_all x1, starting transfers between devices, per_device(): early = lax.all_to_all(packed, path_axes, 0, 0, tiled=True)  23 us
    ppermute x4, starting transfers between devices, hop(): return lax.ppermute(values, fsdp_axes, ways)  17.1 us
    ppermute x4, waiting for transfers between devices, hop(): return lax.ppermute(values, fsdp_axes, ways)  9.45 us
    pallas_call x1, Pallas kernels, per_device(): pl.pallas_call(module_kernel, out_shape=(jax.ShapeDtypeStruct(shape, jnp....  3.91 us
    ppermute x2, starting transfers between devices, swap(): return lax.ppermute(values, 'core', [(0, 1), (1, 0)])  3.84 us
    pallas_call x1, Pallas kernels, per_device(): pl.pallas_call(gradient_kernel, out_shape=jax.ShapeDtypeStruct((stations,...  3.51 us
    ppermute x2, waiting for transfers between devices, swap(): return lax.ppermute(values, 'core', [(0, 1), (1, 0)])  3.43 us
  transfers between devices with their start and end apart: 7, of which 5 were waited for; matrix products, arithmetic and copies ran while one was open for 0% of the time, Pallas kernels for 3%

profile of v4, /device:TPU:16, one launch (start us, length us, event | category | flops | bytes accessed | tf_op | source)
XLA Modules:
  0.0 100.3 jit_solution(4840701325624142329)
XLA Ops:
  0.6 2.4 %pack.1 = bf16[64,96,128]{2,1,0:T(8,128)(2,1)} custom-call(bf16[64,32,128]{2,1,0:T(8,128)(2,1)} %bitcast.16, bf16[64,32,128]{2,1,0:T(8,128)(2,1)} %bitcast.20, bf16[64,32,128]{2,1,0:T(8,128)(2,1)} %bitcast.21), custom_call_target="tpu_custom_call" | custom-call | bytes 3145728 | tf_op jit(solution)/shard_map/pack/pallas_call | solution.py:219
  3.1 0.0 copy-start.2
  3.1 23.0 %all-to-all-start = ((bf16[64,96,128]{2,1,0:T(8,128)(2,1)}), bf16[64,96,128]{2,1,0:T(8,128)(2,1)}, u32[]{:S(2)}, u32[]{:S(2)}) async-start(bf16[64,96,128]{2,1,0:T(8,128)(2,1)} %pack.1), calls=%async_computation | async-start | bytes 3145728 | tf_op jit(solution)/shard_map/all_to_all | solution.py:242
  26.1 0.0 copy-start.3
  26.1 1.9 %collective-permute-start = (bf16[512,128]{1,0:T(8,128)(2,1)S(1)}, bf16[512,128]{1,0:T(8,128)(2,1)S(1)}, u32[]{:S(2)}, u32[]{:S(2)}) collective-permute-start(bf16[512,128]{1,0:T(8,128)(2,1)S(1)} %copy-done.2), channel_id=1, source_target_pairs={{0,1},{1,0},{2,3},{3,2},{4,5},{5,4},{6,7},{7,6},{8,9},{9,8},{10,11... | collective-permute-start | bytes 393224 | tf_op jit(solution)/shard_map/ppermute | solution.py:212
  28.0 1.3 %collective-permute-done = bf16[512,128]{1,0:T(8,128)(2,1)S(1)} collective-permute-done((bf16[512,128]{1,0:T(8,128)(2,1)S(1)}, bf16[512,128]{1,0:T(8,128)(2,1)S(1)}, u32[]{:S(2)}, u32[]{:S(2)}) %collective-permute-start) | collective-permute-done | bytes 131104 | tf_op jit(solution)/shard_map/ppermute | solution.py:212
  29.4 3.6 %collective-permute-start.1 = (bf16[2,512,128]{2,1,0:T(8,128)(2,1)S(1)}, bf16[2,512,128]{2,1,0:T(8,128)(2,1)S(1)}, u32[]{:S(2)}, u32[]{:S(2)}) collective-permute-start(bf16[2,512,128]{2,1,0:T(8,128)(2,1)S(1)} %pad_maximum_fusion.1.chip), channel_id=1, source_target_pairs={{0,2},{2,4},{4,6},{6,8},{8,10},{10,12},{12,14},{14,0},{1,15},{3,1}... | collective-permute-start | bytes 786440 | tf_op jit(solution)/shard_map/ppermute | solution.py:217
  33.0 5.9 %collective-permute-start.2 = (bf16[2,512,128]{2,1,0:T(8,128)(2,1)S(1)}, bf16[2,512,128]{2,1,0:T(8,128)(2,1)S(1)}, u32[]{:S(2)}, u32[]{:S(2)}) collective-permute-start(bf16[2,512,128]{2,1,0:T(8,128)(2,1)S(1)} %pad_maximum_fusion.1.chip), channel_id=1, source_target_pairs={{0,4},{2,6},{4,8},{6,10},{8,12},{10,14},{12,0},{14,2},{1,13},{3,15... | collective-permute-start | bytes 786440 | tf_op jit(solution)/shard_map/ppermute | solution.py:217
  38.9 0.0 collective-permute-done.1
  38.9 3.8 %collective-permute-start.3 = (bf16[2,512,128]{2,1,0:T(8,128)(2,1)S(1)}, bf16[2,512,128]{2,1,0:T(8,128)(2,1)S(1)}, u32[]{:S(2)}, u32[]{:S(2)}) collective-permute-start(bf16[2,512,128]{2,1,0:T(8,128)(2,1)S(1)} %collective-permute-done.1), channel_id=1, source_target_pairs={{0,4},{2,6},{4,8},{6,10},{8,12},{10,14},{12,0},{14,2},{1,13},{3,15... | collective-permute-start | bytes 786440 | tf_op jit(solution)/shard_map/ppermute | solution.py:217
  42.8 0.0 copy-start
  42.8 0.0 copy-start.1
  42.8 3.4 %collective-permute-done.2 = bf16[2,512,128]{2,1,0:T(8,128)(2,1)S(1)} collective-permute-done((bf16[2,512,128]{2,1,0:T(8,128)(2,1)S(1)}, bf16[2,512,128]{2,1,0:T(8,128)(2,1)S(1)}, u32[]{:S(2)}, u32[]{:S(2)}) %collective-permute-start.2) | collective-permute-done | bytes 262176 | tf_op jit(solution)/shard_map/ppermute | solution.py:217
  46.2 3.8 %collective-permute-start.4 = (bf16[2,256,128]{2,1,0:T(8,128)(2,1)S(1)}, bf16[2,256,128]{2,1,0:T(8,128)(2,1)S(1)}, u32[]{:S(2)}, u32[]{:S(2)}) collective-permute-start(bf16[2,256,128]{2,1,0:T(8,128)(2,1)S(1)} %constant_dynamic-slice_fusion), channel_id=1, source_target_pairs={{0,4},{2,6},{4,8},{6,10},{8,12},{10,14},{12,0},{14,2},{1,13},{3,15... | collective-permute-start | bytes 393224 | tf_op jit(solution)/shard_map/ppermute | solution.py:217
  49.9 6.1 %collective-permute-done.4 = bf16[2,256,128]{2,1,0:T(8,128)(2,1)S(1)} collective-permute-done((bf16[2,256,128]{2,1,0:T(8,128)(2,1)S(1)}, bf16[2,256,128]{2,1,0:T(8,128)(2,1)S(1)}, u32[]{:S(2)}, u32[]{:S(2)}) %collective-permute-start.4) | collective-permute-done | bytes 131104 | tf_op jit(solution)/shard_map/ppermute | solution.py:217
  56.0 0.1 pad_maximum_fusion.near
  56.1 1.9 %collective-permute-start.5 = (bf16[3584,128]{1,0:T(8,128)(2,1)S(1)}, bf16[3584,128]{1,0:T(8,128)(2,1)S(1)}, u32[]{:S(2)}, u32[]{:S(2)}) collective-permute-start(bf16[3584,128]{1,0:T(8,128)(2,1)S(1)} %pad_maximum_fusion.near), channel_id=1, source_target_pairs={{0,1},{1,0},{2,3},{3,2},{4,5},{5,4},{6,7},{7,6},{8,9},{9,8},{10,11... | collective-permute-start | bytes 2752520 | tf_op jit(solution)/shard_map/ppermute | solution.py:212
  58.0 0.1 pad_add_fusion.place
  58.1 0.2 fusion.onehot
  58.3 2.1 %collective-permute-done.5.far = bf16[3584,128]{1,0:T(8,128)(2,1)S(1)} collective-permute-done((bf16[3584,128]{1,0:T(8,128)(2,1)S(1)}, bf16[3584,128]{1,0:T(8,128)(2,1)S(1)}, u32[]{:S(2)}, u32[]{:S(2)}) %collective-permute-start.5) | collective-permute-done | bytes 917536 | tf_op jit(solution)/shard_map/ppermute | solution.py:212
  60.5 3.5 %path_gradient.1 = bf16[8,2,128,128]{3,2,1,0:T(8,128)(2,1)S(1)} custom-call(s32[2]{0:T(128)S(1)} %pad_add_fusion.place, bf16[2,512,128]{2,1,0:T(8,128)(2,1)S(1)} %pad_maximum_fusion.1.chip, bf16[3584,128]{1,0:T(8,128)(2,1)S(1)} %pad_maximum_fusion.near, bf16[3584,128]{1,0:T(8,128)(2,1)S(1)} %collective-permute-done.5.far, bf16[1024,512]{1,0:T(8,128)(2,1)S(1)} %fusion.onehot, ...), custom_call_target="tpu_custom_call" | custom-call | flops 2000000000 | bytes 5242880 | tf_op jit(solution)/shard_map/path_gradient/pallas_call | solution.py:249
  64.0 3.2 %all-to-all-done.early_held = bf16[64,96,128]{2,1,0:T(8,128)(2,1)} async-done(((bf16[64,96,128]{2,1,0:T(8,128)(2,1)}), bf16[64,96,128]{2,1,0:T(8,128)(2,1)}, u32[]{:S(2)}, u32[]{:S(2)}) %all-to-all-start) | async-done | bytes 1572896 | tf_op jit(solution)/shard_map/all_to_all | solution.py:242
  67.2 29.2 %all_to_all.10.late_held = bf16[64,32,128]{2,1,0:T(8,128)(2,1)} all-to-all(bf16[64,32,128]{2,1,0:T(8,128)(2,1)S(1)} %bitcast.15), channel_id=1, replica_groups=mesh['z'=8,'x'=8,'y'=8,'core'=2] {'z','x'}, dimensions={0} | all-to-all | bytes 1048576 | tf_op jit(solution)/shard_map/all_to_all | solution.py:262
  96.4 3.9 %module_update.1 = (f32[16,32,128]{2,1,0:T(8,128)}, f32[16,32,128]{2,1,0:T(8,128)}, bf16[16,32,128]{2,1,0:T(8,128)(2,1)}, bf16[16,32,128]{2,1,0:T(8,128)(2,1)}) custom-call(s32[64]{0:T(128)} %table.1, bf16[64,96,128]{2,1,0:T(8,128)(2,1)} %all-to-all-done.early_held, bf16[64,32,128]{2,1,0:T(8,128)(2,1)} %all_to_all.10.late_held, f32[16,32,128]{2,1,0:T(8,128)} %master_held.1, ...), custom_call_target="tpu_custom_call" | custom-call | flops 10000000 | bytes 4194304 | tf_op jit(solution)/shard_map/module_update/pallas_call | solution.py:265
  (7 shorter events, 0.0 us)
Async XLA Ops:
  3.1 23.0 %copy-start.2 = (bf16[512,128]{1,0:T(8,128)(2,1)S(1)}, bf16[512,128]{1,0:T(8,128)(2,1)}, u32[]{:S(2)}) copy-start(bf16[512,128]{1,0:T(8,128)(2,1)} %param.9) | copy-start | bytes 393220
  3.1 64.1 %all-to-all-start = ((bf16[64,96,128]{2,1,0:T(8,128)(2,1)}), bf16[64,96,128]{2,1,0:T(8,128)(2,1)}, u32[]{:S(2)}, u32[]{:S(2)}) async-start(bf16[64,96,128]{2,1,0:T(8,128)(2,1)} %pack.1), calls=%async_computation | async-start | bytes 3145728 | tf_op jit(solution)/shard_map/all_to_all | solution.py:242
  26.1 32.0 %copy-start.3 = (s32[1,1024]{1,0:T(1,128)S(1)}, s32[1,1024]{1,0:T(1,128)}, u32[]{:S(2)}) copy-start(s32[1,1024]{1,0:T(1,128)} %param.10) | copy-start | bytes 12292
  26.1 3.2 %collective-permute-start = (bf16[512,128]{1,0:T(8,128)(2,1)S(1)}, bf16[512,128]{1,0:T(8,128)(2,1)S(1)}, u32[]{:S(2)}, u32[]{:S(2)}) collective-permute-start(bf16[512,128]{1,0:T(8,128)(2,1)S(1)} %copy-done.2), channel_id=1, source_target_pairs={{0,1},{1,0},{2,3},{3,2},{4,5},{5,4},{6,7},{7,6},{8,9},{9,8},{10,11... | collective-permute-start | bytes 393224 | tf_op jit(solution)/shard_map/ppermute | solution.py:212
  29.4 9.6 %collective-permute-start.1 = (bf16[2,512,128]{2,1,0:T(8,128)(2,1)S(1)}, bf16[2,512,128]{2,1,0:T(8,128)(2,1)S(1)}, u32[]{:S(2)}, u32[]{:S(2)}) collective-permute-start(bf16[2,512,128]{2,1,0:T(8,128)(2,1)S(1)} %pad_maximum_fusion.1.chip), channel_id=1, source_target_pairs={{0,2},{2,4},{4,6},{6,8},{8,10},{10,12},{12,14},{14,0},{1,15},{3,1}... | collective-permute-start | bytes 786440 | tf_op jit(solution)/shard_map/ppermute | solution.py:217
  33.0 13.2 %collective-permute-start.2 = (bf16[2,512,128]{2,1,0:T(8,128)(2,1)S(1)}, bf16[2,512,128]{2,1,0:T(8,128)(2,1)S(1)}, u32[]{:S(2)}, u32[]{:S(2)}) collective-permute-start(bf16[2,512,128]{2,1,0:T(8,128)(2,1)S(1)} %pad_maximum_fusion.1.chip), channel_id=1, source_target_pairs={{0,4},{2,6},{4,8},{6,10},{8,12},{10,14},{12,0},{14,2},{1,13},{3,15... | collective-permute-start | bytes 786440 | tf_op jit(solution)/shard_map/ppermute | solution.py:217
  38.9 17.1 %collective-permute-start.3 = (bf16[2,512,128]{2,1,0:T(8,128)(2,1)S(1)}, bf16[2,512,128]{2,1,0:T(8,128)(2,1)S(1)}, u32[]{:S(2)}, u32[]{:S(2)}) collective-permute-start(bf16[2,512,128]{2,1,0:T(8,128)(2,1)S(1)} %collective-permute-done.1), channel_id=1, source_target_pairs={{0,4},{2,6},{4,8},{6,10},{8,12},{10,14},{12,0},{14,2},{1,13},{3,15... | collective-permute-start | bytes 786440 | tf_op jit(solution)/shard_map/ppermute | solution.py:217
  42.8 17.7 %copy-start = (bf16[1,2048,128]{2,1,0:T(8,128)(2,1)S(1)}, bf16[1,2048,128]{2,1,0:T(8,128)(2,1)}, u32[]{:S(2)}) copy-start(bf16[1,2048,128]{2,1,0:T(8,128)(2,1)} %param.13) | copy-start | bytes 1572868
  42.8 17.7 %copy-start.1 = (bf16[1,1024,128]{2,1,0:T(8,128)(2,1)S(1)}, bf16[1,1024,128]{2,1,0:T(8,128)(2,1)}, u32[]{:S(2)}) copy-start(bf16[1,1024,128]{2,1,0:T(8,128)(2,1)} %param.12) | copy-start | bytes 786436
  46.2 9.9 %collective-permute-start.4 = (bf16[2,256,128]{2,1,0:T(8,128)(2,1)S(1)}, bf16[2,256,128]{2,1,0:T(8,128)(2,1)S(1)}, u32[]{:S(2)}, u32[]{:S(2)}) collective-permute-start(bf16[2,256,128]{2,1,0:T(8,128)(2,1)S(1)} %constant_dynamic-slice_fusion), channel_id=1, source_target_pairs={{0,4},{2,6},{4,8},{6,10},{8,12},{10,14},{12,0},{14,2},{1,13},{3,15... | collective-permute-start | bytes 393224 | tf_op jit(solution)/shard_map/ppermute | solution.py:217
  56.1 4.4 %collective-permute-start.5 = (bf16[3584,128]{1,0:T(8,128)(2,1)S(1)}, bf16[3584,128]{1,0:T(8,128)(2,1)S(1)}, u32[]{:S(2)}, u32[]{:S(2)}) collective-permute-start(bf16[3584,128]{1,0:T(8,128)(2,1)S(1)} %pad_maximum_fusion.near), channel_id=1, source_target_pairs={{0,1},{1,0},{2,3},{3,2},{4,5},{5,4},{6,7},{7,6},{8,9},{9,8},{10,11... | collective-permute-start | bytes 2752520 | tf_op jit(solution)/shard_map/ppermute | solution.py:212
